TPU v7x, 512 devices: a whole 4x8x8 slice. The times are simulated.
512 devices in a mesh: gx: 128 (over z, y, core), gy: 4 (over x).
Axes of the slice: x: 4, y: 8, z: 8, core: 2. Of those that a mesh axis runs over, the one named last changes fastest.
Arguments:
- jitter: float32 [3, 1024, 32, 128], P(None, 'gx', 'gy'), may hold values from -0.3 to 0.3
- colour: float32 [1024, 32, 128], P('gx', 'gy'), may hold values from 0 to 1
- surface_cells: int32 [128, 4, 192], P('gx', 'gy'), may hold values from 0 to 8191, as said below
- neighbours: int32 [128, 4, 192, 128], P('gx', 'gy'), may hold values from 0 to 342, as said below
- counts: int32 [128, 4], P('gx', 'gy'), may hold values from 1 to 192, as said below
- pressure: float32 [1024, 32, 128], P('gx', 'gy'), may hold values from -6 to 6
- source: float32 [1024, 32, 128], P('gx', 'gy'), may hold values from -6 to 6
Outputs:
- pressure_out: float32 [1024, 32, 128], P('gx', 'gy')
- curvature_out: float32 [128, 4, 192], P('gx', 'gy')
Inputs may be any that keep to these rules, and one draw needn't show every extreme that they name: `surface_cells`: the cells of one tile's list are distinct. `neighbours`: each code names a step of -3 to 3 lattice cells along every dimension. Among the tiles that share a gx index the counts sum to exactly 256, and one of them has 192.
All inputs are finite; a program needn't handle non-finite values.
Results may differ from a plain program's by a relative error of at most 0.0003.
Values sent between devices are 32-bit elements; how exact they have to be, the bound alone decides.
No kernel may reach another device: no remote copies, remote signals or barrier semaphores. Data moves between devices by JAX's collectives and lax.ppermute only.
A program may use at most 64 MiB of HBM per device.

v0:
```python
import jax
import jax.numpy as jnp
from jax import lax
from jax.sharding import PartitionSpec as P

SMEAN = 64
SWEEPS = 3


SIGMA = 1.0
SMOOTH_SQ = 4.0


def with_halo(value, sides, width):
    for axis, dim in sides:
        size, length = (lax.axis_size(axis), value.shape[dim])
        up = [(i, (i + 1) % size) for i in range(size - 1)]
        down = [(j, i) for i, j in up]
        last = lax.slice_in_dim(value, length - width, length, axis=dim)
        initial = lax.slice_in_dim(value, 0, width, axis=dim)
        before = lax.ppermute(last, axis, up)
        after = lax.ppermute(initial, axis, down)
        value = jnp.concatenate([before, value, after], axis=dim)
    return value


def lattice(size_x, size_y, size_z):
    indices = jnp.arange(size_x * size_y * size_z, dtype=jnp.int32)
    coord_x = (indices // (size_y * size_z)).astype(jnp.float32)
    coord_y = (indices // size_z % size_y).astype(jnp.float32)
    coord_z = (indices % size_z).astype(jnp.float32)
    return jnp.stack([coord_x, coord_y, coord_z])


def decode(cells, codes, size_x, size_y, size_z):
    base_x = (cells // (size_y * size_z))[:, None]
    base_y = (cells // size_z % size_y)[:, None]
    base_z = (cells % size_z)[:, None]
    near_x = jnp.clip(base_x + codes // 49 - 3, 0, size_x - 1)
    near_y = jnp.clip(base_y + codes // 7 % 7 - 3, 0, size_y - 1)
    near_z = jnp.clip(base_z + codes % 7 - 3, 0, size_z - 1)
    return (near_x * size_y + near_y) * size_z + near_z


def owner_rows(jitter_tile, colour_tile, cells, codes, count, size_x, size_y, size_z):
    neighbours = decode(cells, codes, size_x, size_y, size_z)
    places = lattice(size_x, size_y, size_z) + jitter_tile
    centre = places[:, cells]
    beside_all = places[:, neighbours]
    offsets = beside_all - centre[:, :, None]
    shade = colour_tile[neighbours] - colour_tile[cells][:, None]
    stacked = jnp.stack([offsets[0], offsets[1], offsets[2], shade], axis=1)
    live = jnp.arange(cells.shape[0], dtype=jnp.int32) < count
    return jnp.where(live[:, None, None], stacked, jnp.zeros_like(stacked))


def curvature(stacked):
    off_x = stacked[:, 0]
    off_y = stacked[:, 1]
    off_z = stacked[:, 2]
    shade = stacked[:, 3]
    weight = shade * jnp.exp(-(off_x * off_x + off_y * off_y + off_z * off_z) / SMOOTH_SQ)
    first = -2.0 / SMOOTH_SQ
    second = 4.0 / (SMOOTH_SQ * SMOOTH_SQ)
    grad_x = first * jnp.sum(weight * off_x, axis=1)
    grad_y = first * jnp.sum(weight * off_y, axis=1)
    grad_z = first * jnp.sum(weight * off_z, axis=1)
    total = jnp.sum(weight, axis=1)
    hess_xx = second * jnp.sum(weight * off_x * off_x, axis=1) + first * total
    hess_yy = second * jnp.sum(weight * off_y * off_y, axis=1) + first * total
    hess_zz = second * jnp.sum(weight * off_z * off_z, axis=1) + first * total
    hess_xy = second * jnp.sum(weight * off_x * off_y, axis=1)
    hess_xz = second * jnp.sum(weight * off_x * off_z, axis=1)
    hess_yz = second * jnp.sum(weight * off_y * off_z, axis=1)
    trace = hess_xx + hess_yy + hess_zz
    quad = grad_x * grad_x * hess_xx + grad_y * grad_y * hess_yy + grad_z * grad_z * hess_zz
    quad = quad + 2.0 * (
        grad_x * grad_y * hess_xy + grad_x * grad_z * hess_xz + grad_y * grad_z * hess_yz
    )
    denom = 1.0 + grad_x * grad_x + grad_y * grad_y + grad_z * grad_z
    return -(trace - quad / denom) / jnp.sqrt(denom)


def settle(block):
    return curvature(jnp.sum(block, axis=0))


def neighbour_sum(padded):
    beside = padded[2:, 1:-1, 1:-1] + padded[:-2, 1:-1, 1:-1]
    beside = beside + padded[1:-1, 2:, 1:-1] + padded[1:-1, :-2, 1:-1]
    beside = beside + padded[1:-1, 1:-1, 2:] + padded[1:-1, 1:-1, :-2]
    return beside


def first_row(every_count, position, group):
    below = jnp.arange(group, dtype=jnp.int32) < position
    return jnp.sum(jnp.where(below, every_count, 0))


def spread_rows(rows, start, column, group):
    empty = jnp.zeros((column + rows.shape[0],) + rows.shape[1:], rows.dtype)
    placed = lax.dynamic_update_slice_in_dim(empty, rows, start, 0)[:column]
    return placed.reshape((group, column // group) + rows.shape[1:])


def own_slice(gathered, start, slots):
    longer = jnp.concatenate([gathered, jnp.zeros((slots,), jnp.float32)])
    return lax.dynamic_slice_in_dim(longer, start, slots, 0)


def per_device(jitter, colour, surface_cells, neighbours, counts, pressure, source):
    size_x, size_y, size_z = colour.shape
    count = counts[0, 0]
    cells = surface_cells[0, 0]
    slots = cells.shape[0]
    live = jnp.arange(slots, dtype=jnp.int32) < count
    stacked = owner_rows(
        jitter.reshape(3, -1),
        colour.reshape(-1),
        cells,
        neighbours[0, 0],
        count,
        size_x,
        size_y,
        size_z,
    )
    group = lax.axis_size("gy")
    every_count = lax.all_gather(counts[0], "gy", axis=0, tiled=True)
    start = first_row(every_count, lax.axis_index("gy"), group)
    column = group * SMEAN
    spread = spread_rows(stacked, start, column, group)
    balanced = settle(lax.all_to_all(spread, "gy", split_axis=0, concat_axis=0, tiled=True))
    gathered = lax.all_gather(balanced, "gy", axis=0, tiled=True)
    values = own_slice(gathered, start, slots)
    kappa = jnp.where(live, values, jnp.zeros_like(values))
    rhs = source.reshape(-1).at[cells].add(SIGMA * kappa).reshape(source.shape)
    current = pressure
    for sweep in range(SWEEPS):
        padded = with_halo(current, (("gx", 0), ("gy", 1)), 1)
        padded = jnp.pad(padded, ((0, 0), (0, 0), (1, 1)))
        current = (neighbour_sum(padded) + rhs) / 6.0
    return (current, kappa[None, None, :])


def solution(mesh):
    placed = (
        P(None, "gx", "gy", None),
        P("gx", "gy", None),
        P("gx", "gy", None),
        P("gx", "gy", None, None),
        P("gx", "gy"),
        P("gx", "gy", None),
        P("gx", "gy", None),
    )
    return jax.shard_map(
        per_device,
        mesh=mesh,
        in_specs=placed,
        out_specs=(P("gx", "gy", None), P("gx", "gy", None)),
        check_vma=False,
    )
```

profile of v0, /device:TPU:260, one launch (start us, length us, event | category | flops | bytes accessed | tf_op | source)
XLA Modules:
  0.0 337.9 jit_solution(11178519359666646886)
XLA Ops:
  0.6 0.0 copy-start
  0.7 0.7 fusion.50
  1.4 1.9 collective-permute-start.1
  3.3 0.1 fusion.20
  3.4 0.7 compare_select_fusion.3
  4.1 0.7 and_select_fusion.7
  4.8 0.1 pad_maximum_fusion
  4.9 2.7 copy.27
  7.6 2.6 copy.26
  10.2 5.9 %bitcast_add_fusion = f32[3,8192]{0,1:T(8,128)} fusion(f32[3,8192]{0,1:T(8,128)} %copy.27, f32[3,8,8,128]{0,3,2,1:T(8,128)} %copy.26), kind=kLoop, calls=%fused_computation.5 | loop fusion | flops 24576 | bytes 294912 | tf_op jit(solution)/shard_map/add | solution.py:47
  16.0 0.3 bitcast_clamp_fusion
  16.4 83.5 %gather_fusion = f32[24576,3]{1,0:T(8,128)} fusion(f32[3,8192]{0,1:T(8,128)} %bitcast_add_fusion, s32[24576]{0:T(1024)S(1)} %bitcast_clamp_fusion), kind=kCustom, calls=%fused_computation | custom fusion | bytes 688128 | tf_op jit(solution)/shard_map/gather | solution.py:49
  99.8 7.5 %copy.28 = f32[192,128,3]{1,0,2:T(8,128)S(1)} copy(f32[192,128,3]{2,1,0:T(8,128)} %bitcast.120) | data formatting | bytes 589824 | tf_op jit(solution)/shard_map/gather | solution.py:49
  107.3 2.9 gather_fusion.1
  110.2 0.1 copy.29
  110.3 0.2 bitcast_subtract_fusion
  110.5 135.5 %gather_fusion.2 = f32[24576]{0:T(1024)S(1)} fusion(f32[8192]{0:T(1024)S(1)} %bitcast.117, s32[24576]{0:T(1024)S(1)} %bitcast_clamp_fusion), kind=kCustom, calls=%fused_computation.2 | custom fusion | bytes 294912 | tf_op jit(solution)/shard_map/gather | solution.py:51
  246.0 0.0 copy-start.2
  246.0 0.0 copy-start.1
  246.7 1.3 dynamic-slice
  248.0 0.7 bitcast_dynamic-update-slice_fusion
  248.7 1.4 gather_fusion.3
  250.1 6.4 %all-reduce.4 = s32[4]{0:T(128)S(1)} all-reduce(s32[4]{0:T(128)S(1)} %bitcast_dynamic-update-slice_fusion), channel_id=2, replica_groups=mesh['gx'=128,'gy'=4] {'gy'}, use_global_device_ids=true, to_apply=%add.4 | all-reduce | flops 4 | bytes 32 | tf_op jit(solution)/shard_map/all_gather | solution.py:128
  256.5 0.1 bitcast_subtract_fusion.1
  256.6 0.1 maximum_select_fusion
  256.7 0.7 fusion.44
  259.5 0.1 broadcast_in_dim.14
  259.6 3.1 dynamic_update_slice.3
  262.7 0.8 copy.30
  263.6 7.9 %all-to-all-start = ((f32[4,64,4,128]{3,1,2,0:T(8,128)}), f32[4,64,4,128]{3,1,2,0:T(8,128)S(1)}, u32[]{:S(2)}, u32[]{:S(2)}) async-start(f32[4,64,4,128]{3,1,2,0:T(8,128)} %copy.30), calls=%async_computation | async-start | bytes 1048576 | tf_op jit(solution)/shard_map/all_to_all | solution.py:132
  271.5 4.9 %collective-permute-start = (f32[1,8,128]{2,1,0:T(8,128)S(1)}, f32[1,8,128]{2,1,0:T(8,128)S(1)}, u32[]{:S(2)}, u32[]{:S(2)}) collective-permute-start(f32[1,8,128]{2,1,0:T(8,128)S(1)} %get-tuple-element.32), channel_id=1, source_target_pairs={{4,0},{8,4},{12,8},{16,12},{20,16},{24,20},{28,24},{32,28},{36,32}... | collective-permute-start | bytes 12296 | tf_op jit(solution)/shard_map/ppermute | solution.py:22
  276.4 0.0 collective-permute-done.1
  276.5 1.3 collective-permute-done
  277.7 2.5 collective-permute-start.2
  280.2 3.4 collective-permute-start.3
  284.2 0.0 collective-permute-done.2
  284.2 1.5 collective-permute-done.3
  285.7 0.1 select_maximum_fusion.8
  285.9 0.0 all-to-all-done
  285.9 0.3 multiply_reduce_fusion.5
  286.2 0.1 multiply_dynamic-update-slice_fusion
  286.3 8.6 %all-reduce.5 = f32[256]{0:T(256)S(1)} all-reduce(f32[256]{0:T(256)S(1)} %multiply_dynamic-update-slice_fusion), channel_id=1, replica_groups=mesh['gx'=128,'gy'=4] {'gy'}, use_global_device_ids=true, to_apply=%add.5 | all-reduce | flops 256 | bytes 2048
  294.9 0.1 fusion.42
  295.0 1.6 scatter_fusion
  296.6 0.1 fusion.36
  296.7 3.5 %collective-permute-start.4 = (f32[1,8,128]{2,1,0:T(8,128)S(1)}, f32[1,8,128]{2,1,0:T(8,128)S(1)}, u32[]{:S(2)}, u32[]{:S(2)}) collective-permute-start(f32[1,8,128]{2,1,0:T(8,128)S(1)} %get-tuple-element.31), channel_id=1, source_target_pairs={{4,0},{8,4},{12,8},{16,12},{20,16},{24,20},{28,24},{32,28},{36,32}... | collective-permute-start | bytes 12296 | tf_op jit(solution)/shard_map/ppermute | solution.py:22
  300.2 1.9 collective-permute-start.5
  302.1 0.0 collective-permute-done.4
  302.2 6.3 %collective-permute-done.5 = f32[1,8,128]{2,1,0:T(8,128)S(1)} collective-permute-done((f32[1,8,128]{2,1,0:T(8,128)S(1)}, f32[1,8,128]{2,1,0:T(8,128)S(1)}, u32[]{:S(2)}, u32[]{:S(2)}) %collective-permute-start.5) | collective-permute-done | bytes 4128 | tf_op jit(solution)/shard_map/ppermute | solution.py:21
  308.5 2.5 collective-permute-start.6
  311.0 3.4 collective-permute-start.7
  314.3 0.0 collective-permute-done.6
  314.3 2.8 collective-permute-done.7
  317.1 0.2 select_maximum_fusion.4
  317.3 0.1 fusion.30
  317.4 1.9 collective-permute-start.8
  319.3 2.4 collective-permute-start.9
  321.7 0.0 collective-permute-done.8
  321.7 5.8 %collective-permute-done.9 = f32[1,8,128]{2,1,0:T(8,128)S(1)} collective-permute-done((f32[1,8,128]{2,1,0:T(8,128)S(1)}, f32[1,8,128]{2,1,0:T(8,128)S(1)}, u32[]{:S(2)}, u32[]{:S(2)}) %collective-permute-start.9) | collective-permute-done | bytes 4128 | tf_op jit(solution)/shard_map/ppermute | solution.py:21
  327.6 3.9 %collective-permute-start.10 = (f32[10,1,128]{2,1,0:T(1,128)S(1)}, f32[10,1,128]{2,1,0:T(1,128)S(1)}, u32[]{:S(2)}, u32[]{:S(2)}) collective-permute-start(f32[10,1,128]{2,1,0:T(1,128)S(1)} %get-tuple-element.23), channel_id=1, source_target_pairs={{1,0},{2,1},{3,2},{5,4},{6,5},{7,6},{9,8},{10,9},{11,10},{13,12},{... | collective-permute-start | bytes 15368 | tf_op jit(solution)/shard_map/ppermute | solution.py:22
  331.5 1.9 collective-permute-start.11
  333.4 3.6 %collective-permute-done.11 = f32[10,1,128]{2,1,0:T(1,128)S(1)} collective-permute-done((f32[10,1,128]{2,1,0:T(1,128)S(1)}, f32[10,1,128]{2,1,0:T(1,128)S(1)}, u32[]{:S(2)}, u32[]{:S(2)}) %collective-permute-start.11) | collective-permute-done | bytes 5152 | tf_op jit(solution)/shard_map/ppermute | solution.py:21
  337.0 0.2 select_maximum_fusion
  337.2 0.7 fusion.25
  (27 shorter events, 0.2 us)
Async XLA Ops:
  0.6 109.8 %copy-start = (f32[8,8,128]{2,1,0:T(8,128)S(1)}, f32[8,8,128]{2,1,0:T(8,128)}, u32[]{:S(2)}) copy-start(f32[8,8,128]{2,1,0:T(8,128)} %param.8) | copy-start | bytes 98308
  0.6 6.9 %copy-start.4 = (f32[3,8,8,128]{3,2,1,0:T(8,128)S(1)}, f32[3,8,8,128]{3,2,1,0:T(8,128)}, u32[]{:S(2)}) copy-start(f32[3,8,8,128]{3,2,1,0:T(8,128)} %param.7) | copy-start | bytes 294916
  1.4 275.0 %collective-permute-start.1 = (f32[1,8,128]{2,1,0:T(8,128)S(1)}, f32[1,8,128]{2,1,0:T(8,128)S(1)}, u32[]{:S(2)}, u32[]{:S(2)}) collective-permute-start(f32[1,8,128]{2,1,0:T(8,128)S(1)} %get-tuple-element.33), channel_id=1, source_target_pairs={{0,4},{4,8},{8,12},{12,16},{16,20},{20,24},{24,28},{28,32},{32,36}... | collective-permute-start | bytes 12296 | tf_op jit(solution)/shard_map/ppermute | solution.py:21
  10.2 5.9 %copy-start.3 = (s32[1,1,192,128]{3,2,1,0:T(8,128)S(1)}, s32[1,1,192,128]{3,2,1,0:T(8,128)}, u32[]{:S(2)}) copy-start(s32[1,1,192,128]{3,2,1,0:T(8,128)} %param.10) | copy-start | bytes 294916
  246.0 30.4 %copy-start.2 = (f32[8,8,128]{2,1,0:T(8,128)S(1)}, f32[8,8,128]{2,1,0:T(8,128)}, u32[]{:S(2)}) copy-start(f32[8,8,128]{2,1,0:T(8,128)} %param.12) | copy-start | bytes 98308
  246.0 48.9 %copy-start.1 = (f32[8,8,128]{2,1,0:T(8,128)S(1)}, f32[8,8,128]{2,1,0:T(8,128)}, u32[]{:S(2)}) copy-start(f32[8,8,128]{2,1,0:T(8,128)} %param.13) | copy-start | bytes 98308
  263.6 22.3 %all-to-all-start = ((f32[4,64,4,128]{3,1,2,0:T(8,128)}), f32[4,64,4,128]{3,1,2,0:T(8,128)S(1)}, u32[]{:S(2)}, u32[]{:S(2)}) async-start(f32[4,64,4,128]{3,1,2,0:T(8,128)} %copy.30), calls=%async_computation | async-start | bytes 1048576 | tf_op jit(solution)/shard_map/all_to_all | solution.py:132
  271.5 6.3 %collective-permute-start = (f32[1,8,128]{2,1,0:T(8,128)S(1)}, f32[1,8,128]{2,1,0:T(8,128)S(1)}, u32[]{:S(2)}, u32[]{:S(2)}) collective-permute-start(f32[1,8,128]{2,1,0:T(8,128)S(1)} %get-tuple-element.32), channel_id=1, source_target_pairs={{4,0},{8,4},{12,8},{16,12},{20,16},{24,20},{28,24},{32,28},{36,32}... | collective-permute-start | bytes 12296 | tf_op jit(solution)/shard_map/ppermute | solution.py:22
  277.7 6.5 %collective-permute-start.2 = (f32[10,1,128]{2,1,0:T(1,128)S(1)}, f32[10,1,128]{2,1,0:T(1,128)S(1)}, u32[]{:S(2)}, u32[]{:S(2)}) collective-permute-start(f32[10,1,128]{2,1,0:T(1,128)S(1)} %get-tuple-element.27), channel_id=1, source_target_pairs={{1,0},{2,1},{3,2},{5,4},{6,5},{7,6},{9,8},{10,9},{11,10},{13,12},{... | collective-permute-start | bytes 15368 | tf_op jit(solution)/shard_map/ppermute | solution.py:22
  280.2 5.5 %collective-permute-start.3 = (f32[10,1,128]{2,1,0:T(1,128)S(1)}, f32[10,1,128]{2,1,0:T(1,128)S(1)}, u32[]{:S(2)}, u32[]{:S(2)}) collective-permute-start(f32[10,1,128]{2,1,0:T(1,128)S(1)} %get-tuple-element.26), channel_id=1, source_target_pairs={{0,1},{1,2},{2,3},{4,5},{5,6},{6,7},{8,9},{9,10},{10,11},{12,13},{... | collective-permute-start | bytes 15368 | tf_op jit(solution)/shard_map/ppermute | solution.py:21
  295.0 42.9 %copy-start.5 = (f32[192]{0:T(256)}, f32[192]{0:T(256)S(1)}, u32[]{:S(2)}) copy-start(f32[192]{0:T(256)S(1)} %fusion.42) | copy-start | bytes 2308
  296.7 5.4 %collective-permute-start.4 = (f32[1,8,128]{2,1,0:T(8,128)S(1)}, f32[1,8,128]{2,1,0:T(8,128)S(1)}, u32[]{:S(2)}, u32[]{:S(2)}) collective-permute-start(f32[1,8,128]{2,1,0:T(8,128)S(1)} %get-tuple-element.31), channel_id=1, source_target_pairs={{4,0},{8,4},{12,8},{16,12},{20,16},{24,20},{28,24},{32,28},{36,32}... | collective-permute-start | bytes 12296 | tf_op jit(solution)/shard_map/ppermute | solution.py:22
  300.2 8.2 %collective-permute-start.5 = (f32[1,8,128]{2,1,0:T(8,128)S(1)}, f32[1,8,128]{2,1,0:T(8,128)S(1)}, u32[]{:S(2)}, u32[]{:S(2)}) collective-permute-start(f32[1,8,128]{2,1,0:T(8,128)S(1)} %get-tuple-element.30), channel_id=1, source_target_pairs={{0,4},{4,8},{8,12},{12,16},{16,20},{20,24},{24,28},{28,32},{32,36}... | collective-permute-start | bytes 12296 | tf_op jit(solution)/shard_map/ppermute | solution.py:21
  308.5 5.9 %collective-permute-start.6 = (f32[10,1,128]{2,1,0:T(1,128)S(1)}, f32[10,1,128]{2,1,0:T(1,128)S(1)}, u32[]{:S(2)}, u32[]{:S(2)}) collective-permute-start(f32[10,1,128]{2,1,0:T(1,128)S(1)} %get-tuple-element.25), channel_id=1, source_target_pairs={{1,0},{2,1},{3,2},{5,4},{6,5},{7,6},{9,8},{10,9},{11,10},{13,12},{... | collective-permute-start | bytes 15368 | tf_op jit(solution)/shard_map/ppermute | solution.py:22
  311.0 6.2 %collective-permute-start.7 = (f32[10,1,128]{2,1,0:T(1,128)S(1)}, f32[10,1,128]{2,1,0:T(1,128)S(1)}, u32[]{:S(2)}, u32[]{:S(2)}) collective-permute-start(f32[10,1,128]{2,1,0:T(1,128)S(1)} %get-tuple-element.24), channel_id=1, source_target_pairs={{0,1},{1,2},{2,3},{4,5},{5,6},{6,7},{8,9},{9,10},{10,11},{12,13},{... | collective-permute-start | bytes 15368 | tf_op jit(solution)/shard_map/ppermute | solution.py:21
  317.4 4.3 %collective-permute-start.8 = (f32[1,8,128]{2,1,0:T(8,128)S(1)}, f32[1,8,128]{2,1,0:T(8,128)S(1)}, u32[]{:S(2)}, u32[]{:S(2)}) collective-permute-start(f32[1,8,128]{2,1,0:T(8,128)S(1)} %get-tuple-element.29), channel_id=1, source_target_pairs={{4,0},{8,4},{12,8},{16,12},{20,16},{24,20},{28,24},{32,28},{36,32}... | collective-permute-start | bytes 12296 | tf_op jit(solution)/shard_map/ppermute | solution.py:22
  319.3 8.2 %collective-permute-start.9 = (f32[1,8,128]{2,1,0:T(8,128)S(1)}, f32[1,8,128]{2,1,0:T(8,128)S(1)}, u32[]{:S(2)}, u32[]{:S(2)}) collective-permute-start(f32[1,8,128]{2,1,0:T(8,128)S(1)} %get-tuple-element.28), channel_id=1, source_target_pairs={{0,4},{4,8},{8,12},{12,16},{16,20},{20,24},{24,28},{28,32},{32,36}... | collective-permute-start | bytes 12296 | tf_op jit(solution)/shard_map/ppermute | solution.py:21
  327.6 5.9 %collective-permute-start.10 = (f32[10,1,128]{2,1,0:T(1,128)S(1)}, f32[10,1,128]{2,1,0:T(1,128)S(1)}, u32[]{:S(2)}, u32[]{:S(2)}) collective-permute-start(f32[10,1,128]{2,1,0:T(1,128)S(1)} %get-tuple-element.23), channel_id=1, source_target_pairs={{1,0},{2,1},{3,2},{5,4},{6,5},{7,6},{9,8},{10,9},{11,10},{13,12},{... | collective-permute-start | bytes 15368 | tf_op jit(solution)/shard_map/ppermute | solution.py:22
  331.5 5.5 %collective-permute-start.11 = (f32[10,1,128]{2,1,0:T(1,128)S(1)}, f32[10,1,128]{2,1,0:T(1,128)S(1)}, u32[]{:S(2)}, u32[]{:S(2)}) collective-permute-start(f32[10,1,128]{2,1,0:T(1,128)S(1)} %get-tuple-element.22), channel_id=1, source_target_pairs={{0,1},{1,2},{2,3},{4,5},{5,6},{6,7},{8,9},{9,10},{10,11},{12,13},{... | collective-permute-start | bytes 15368 | tf_op jit(solution)/shard_map/ppermute | solution.py:21
where the time goes:
time: 339 us; the launch traced here: 338 us
  local copies, waits for them, and re-layouts  243 us (72%)
  starting transfers between devices  42 us (12%)
  waiting for transfers between devices  21.2 us (6%)
  blocking collectives  14.9 us (4%)
  other arithmetic  12.3 us (4%)
  between operations  4.46 us (1%)
    gather x2, local copies, waits for them, and re-layouts, owner_rows(): shade = colour_tile[neighbours] - colour_tile[cells][:, None]  137 us
    gather x2, local copies, waits for them, and re-layouts, owner_rows(): beside_all = places[:, neighbours]  90.9 us
    ppermute x6, waiting for transfers between devices, with_halo(): before = lax.ppermute(last, axis, up)  20 us
    ppermute x6, starting transfers between devices, with_halo(): after = lax.ppermute(initial, axis, down)  19.2 us
    ppermute x6, starting transfers between devices, with_halo(): before = lax.ppermute(last, axis, up)  14.9 us
    unnamed x1, blocking collectives  8.56 us
    all_to_all x1, starting transfers between devices, per_device(): lax.all_to_all(spread, 'gy', split_axis=0, concat_axis=0, tiled=True)  7.9 us
  transfers between devices with their start and end apart: 13, of which 6 were waited for; matrix products, arithmetic and copies ran while one was open for 74% of the time, Pallas kernels for 0%

commit v1 on v0

v1 whole, which is shorter than its diff:
```python
import functools

import jax
import jax.numpy as jnp
from jax import lax
from jax.experimental import pallas as pl
from jax.experimental.pallas import tpu as pltpu
from jax.sharding import PartitionSpec as P

SIGMA = 1.0
SMOOTH_SQ = 4.0
SLOTS = 192
LANES = 128
ROWS = 64
STEP = 24


def pieces(value):
    high = value.astype(jnp.bfloat16)
    rest = value - high.astype(jnp.float32)
    mid = rest.astype(jnp.bfloat16)
    low = (rest - mid.astype(jnp.float32)).astype(jnp.bfloat16)
    return high, mid, low


def lane_take(table, index):
    return jnp.take_along_axis(table, index, axis=1, mode="promise_in_bounds")


def final_curvature(total, gx, gy, gz, xx, yy, zz, xy, xz, yz):
    first = -2.0 / SMOOTH_SQ
    second = 4.0 / (SMOOTH_SQ * SMOOTH_SQ)
    gx, gy, gz = first * gx, first * gy, first * gz
    xx = second * xx + first * total
    yy = second * yy + first * total
    zz = second * zz + first * total
    xy, xz, yz = second * xy, second * xz, second * yz
    trace = xx + yy + zz
    quad = gx * gx * xx + gy * gy * yy + gz * gz * zz
    quad = quad + 2.0 * (gx * gy * xy + gx * gz * xz + gy * gz * yz)
    denom = 1.0 + gx * gx + gy * gy + gz * gz
    return -(trace - quad / denom) / jnp.sqrt(denom)


def curvature_kernel(
    jitter_ref, colour_ref, cells_ref, codes_ref, counts_ref, source_ref, pressure_ref,
    kappa_ref, rhs_ref, even_ref, odd_ref,
    table, hot, window, place, row, moments,
):
    zero = jnp.zeros((ROWS, LANES), jnp.bfloat16)
    for c in range(4):
        value = colour_ref[...] if c == 3 else jitter_ref[c]
        for q, piece in enumerate(pieces(value.reshape(ROWS, LANES))):
            for p in range(2):
                rows = pl.ds(c * LANES + p * ROWS, ROWS)
                table[q, rows, p * LANES : (p + 1) * LANES] = piece
                table[q, rows, (1 - p) * LANES : (2 - p) * LANES] = zero

    row[...] = jnp.zeros_like(row)
    row[0:1, 0:SLOTS] = cells_ref[0]
    cells_row = row[0:1, :]
    as_float = cells_row.astype(jnp.float32)
    for h in range(2):
        part = jnp.broadcast_to(as_float[:, h * LANES : (h + 1) * LANES], (LANES, LANES))
        turned = part.T.astype(jnp.int32)
        keep = min(LANES, SLOTS - h * LANES)
        place[h * LANES : h * LANES + keep, :] = turned[:keep]

    lane = lax.broadcasted_iota(jnp.int32, (SLOTS, LANES), 1)
    z_of = place[...] & 127
    for step in range(8):
        target = jnp.clip(z_of + (step - 3), 0, LANES - 1)
        d, p = step // 2, step % 2
        hot[d * SLOTS : (d + 1) * SLOTS, p * LANES : (p + 1) * LANES] = jnp.where(
            lane == target, 1.0, 0.0
        ).astype(jnp.bfloat16)

    contract = (((1,), (1,)), ((), ()))
    acc = lax.dot_general(hot[...], table[0], contract, preferred_element_type=jnp.float32)
    acc = acc + lax.dot_general(hot[...], table[1], contract, preferred_element_type=jnp.float32)
    acc = acc + lax.dot_general(hot[...], table[2], contract, preferred_element_type=jnp.float32)
    window[...] = acc

    lane_step = lax.broadcasted_iota(jnp.int32, (STEP, LANES), 1)

    def group(g, carry):
        start = pl.multiple_of(g * STEP, 8)
        rows = pl.ds(start, STEP)
        cell = place[rows, :]
        code = codes_ref[0, 0, rows, :]
        x, y, z = cell >> 10, (cell >> 7) & 7, cell & 127
        a = (code * 1338) >> 16
        rest = code - a * 49
        b = (rest * 9363) >> 16
        dz = rest - b * 7
        near_x = jnp.clip(x + a - 3, 0, 7)
        near_y = jnp.clip(y + b - 3, 0, 7)
        near_z = jnp.clip(z + dz - 3, 0, LANES - 1)
        index = (dz & 1) * ROWS + near_x * 8 + near_y
        centre = ROWS + (cell >> 7)
        d = dz >> 1
        low, first, third = d < 2, d < 1, d < 3
        diff = []
        for c in range(4):
            cols = slice(c * LANES, (c + 1) * LANES)
            tabs = [window[pl.ds(pl.multiple_of(k * SLOTS + start, 8), STEP), cols] for k in range(4)]
            got = [lane_take(t, index) for t in tabs]
            value = jnp.where(
                low, jnp.where(first, got[0], got[1]), jnp.where(third, got[2], got[3])
            )
            diff.append(value - lane_take(tabs[1], centre))
        ox = (near_x - x).astype(jnp.float32) + diff[0]
        oy = (near_y - y).astype(jnp.float32) + diff[1]
        oz = (near_z - z).astype(jnp.float32) + diff[2]
        w = diff[3] * jnp.exp(-(ox * ox + oy * oy + oz * oz) / SMOOTH_SQ)
        wx, wy, wz = w * ox, w * oy, w * oz
        terms = (w, wx, wy, wz, wx * ox, wy * oy, wz * oz, wx * oy, wx * oz, wy * oz)
        out = jnp.zeros((STEP, LANES), jnp.float32)
        for q, term in enumerate(terms):
            out = jnp.where(lane_step == q, jnp.sum(term, axis=1, keepdims=True), out)
        moments[rows, :] = out
        return carry

    moments[SLOTS:, :] = jnp.zeros((2 * LANES - SLOTS, LANES), jnp.float32)
    lax.fori_loop(0, SLOTS // STEP, group, 0)

    sums = jnp.concatenate([moments[0:LANES, :].T, moments[LANES:, :].T], axis=1)
    kappa = final_curvature(*[sums[q : q + 1, :] for q in range(10)])
    slot = lax.broadcasted_iota(jnp.int32, (1, 2 * LANES), 1)
    kappa = jnp.where(slot < counts_ref[0, 0], kappa, 0.0)
    kappa_ref[0] = kappa[:, :SLOTS]

    sub = lax.broadcasted_iota(jnp.int32, (ROWS, 2 * LANES), 0)
    spread = jnp.where(sub == (cells_row >> 7), SIGMA * kappa, 0.0)
    added = jnp.zeros((ROWS, LANES), jnp.float32)
    for piece in pieces(spread):
        added = added + jnp.dot(
            piece[:, :LANES], hot[SLOTS : SLOTS + LANES, LANES:], preferred_element_type=jnp.float32
        )
        added = added + jnp.dot(
            piece[:, LANES:SLOTS], hot[SLOTS + LANES : 2 * SLOTS, LANES:], preferred_element_type=jnp.float32
        )
    rhs = source_ref[...] + added.reshape(8, 8, LANES)
    rhs_ref[...] = rhs
    even = lax.rem(lax.axis_index("gx"), 2) == 0
    pressure = pressure_ref[...]

    def send(ref, high):
        ref[0:3] = jnp.where(high, pressure[5:8], pressure[0:3])
        ref[3:5] = jnp.where(high, rhs[6:8], rhs[0:2])

    send(even_ref, even)
    send(odd_ref, jnp.logical_not(even))


def curvature_call(jitter, colour, cells, codes, counts, source, pressure):
    tile = jax.ShapeDtypeStruct((8, 8, LANES), jnp.float32)
    slab = jax.ShapeDtypeStruct((5, 8, LANES), jnp.float32)
    vmem = pl.BlockSpec(memory_space=pltpu.VMEM)
    smem = pl.BlockSpec(memory_space=pltpu.SMEM)
    return pl.pallas_call(
        curvature_kernel,
        out_shape=(jax.ShapeDtypeStruct((1, 1, SLOTS), jnp.float32), tile, slab, slab),
        in_specs=[vmem, vmem, vmem, vmem, smem, vmem, vmem],
        out_specs=(vmem, vmem, vmem, vmem),
        scratch_shapes=[
            pltpu.VMEM((3, 4 * LANES, 2 * LANES), jnp.bfloat16),
            pltpu.VMEM((4 * SLOTS, 2 * LANES), jnp.bfloat16),
            pltpu.VMEM((4 * SLOTS, 4 * LANES), jnp.float32),
            pltpu.VMEM((SLOTS, LANES), jnp.int32),
            pltpu.VMEM((8, 2 * LANES), jnp.int32),
            pltpu.VMEM((2 * LANES, LANES), jnp.float32),
        ],
        compiler_params=pltpu.CompilerParams(vmem_limit_bytes=32 * 2**20),
        name="curvature",
    )(jitter, colour, cells, codes, counts, source, pressure)


def sides(first, second, even):
    return jnp.where(even, second, first), jnp.where(even, first, second)


def middle_kernel(pressure_ref, rhs_ref, xe_ref, xo_ref, even_ref, odd_ref):
    even_x = lax.rem(lax.axis_index("gx"), 2) == 0
    even_y = lax.rem(lax.axis_index("gy"), 2) == 0
    below, above = sides(xe_ref[...], xo_ref[...], even_x)
    planes = jnp.concatenate([below[1:3], pressure_ref[...], above[0:2]], axis=0)
    rhs = jnp.concatenate([below[3:5], rhs_ref[...], above[3:5]], axis=0)
    sub = lax.broadcasted_iota(jnp.int32, (1, 8, LANES), 1)
    high = jnp.where(sub >= 5, planes, pltpu.roll(rhs, 5, 1))
    low = jnp.where(sub < 3, planes, pltpu.roll(rhs, 3, 1))
    even_ref[...] = jnp.where(even_y, high, low)
    odd_ref[...] = jnp.where(even_y, low, high)


def middle_call(pressure, rhs, xe, xo):
    vmem = pl.BlockSpec(memory_space=pltpu.VMEM)
    strip = jax.ShapeDtypeStruct((12, 8, LANES), jnp.float32)
    return pl.pallas_call(
        middle_kernel,
        out_shape=(strip, strip),
        in_specs=[vmem] * 4,
        out_specs=(vmem, vmem),
        name="edges",
    )(pressure, rhs, xe, xo)


def sweeps_kernel(n_gx, n_gy, pressure_ref, rhs_ref, xe_ref, xo_ref, ye_ref, yo_ref, out_ref):
    at_x, at_y = lax.axis_index("gx"), lax.axis_index("gy")
    below, above = sides(xe_ref[...], xo_ref[...], lax.rem(at_x, 2) == 0)
    left, right = sides(ye_ref[...], yo_ref[...], lax.rem(at_y, 2) == 0)
    own = jnp.concatenate([below[0:3], pressure_ref[...], above[0:3]], axis=0)
    rhs = jnp.concatenate([below[3:5], rhs_ref[...], above[3:5]], axis=0)
    nothing = jnp.zeros((1, 8, LANES), jnp.float32)
    wide_left = jnp.concatenate([nothing, left, nothing], axis=0)
    wide_right = jnp.concatenate([nothing, right, nothing], axis=0)
    current = jnp.concatenate([wide_left, own, wide_right], axis=1)
    rhs = jnp.concatenate([pltpu.roll(left, 3, 1), rhs, pltpu.roll(right, 5, 1)], axis=1)
    lane = lax.broadcasted_iota(jnp.int32, (1, 24, LANES), 2)
    sub = lax.broadcasted_iota(jnp.int32, (1, 24, LANES), 1)
    inside = (jnp.where(at_y > 0, 0, 8) <= sub) & (sub < jnp.where(at_y < n_gy - 1, 24, 16))
    for sweep in range(3):
        mid = current[1:-1]
        beside = current[2:] + current[:-2]
        beside = beside + pltpu.roll(mid, 23, 1) + pltpu.roll(mid, 1, 1)
        beside = beside + jnp.where(lane < LANES - 1, pltpu.roll(mid, LANES - 1, 2), 0.0)
        beside = beside + jnp.where(lane > 0, pltpu.roll(mid, 1, 2), 0.0)
        current = (beside + rhs[sweep : 12 - sweep]) / 6.0
        if sweep < 2:
            count = 12 - 2 * sweep
            plane = lax.broadcasted_iota(jnp.int32, (count, 1, 1), 0) + (sweep - 2)
            held = (plane >= jnp.where(at_x > 0, -2, 0)) & (plane < jnp.where(at_x < n_gx - 1, 10, 8))
            current = jnp.where(held & inside, current, 0.0)
    out_ref[...] = current[:, 8:16, :]


def sweeps_call(n_gx, n_gy, *values):
    vmem = pl.BlockSpec(memory_space=pltpu.VMEM)
    return pl.pallas_call(
        functools.partial(sweeps_kernel, n_gx, n_gy),
        out_shape=jax.ShapeDtypeStruct((8, 8, LANES), jnp.float32),
        in_specs=[vmem] * 6,
        out_specs=vmem,
        name="sweeps",
    )(*values)


def swap(value, axis, odd):
    size = lax.axis_size(axis)
    pairs = []
    for i in range(odd, size - 1, 2):
        pairs += [(i, i + 1), (i + 1, i)]
    return lax.ppermute(value, axis, pairs)


def per_device(jitter, colour, surface_cells, neighbours, counts, pressure, source):
    kappa, rhs, even, odd = curvature_call(
        jitter, colour, surface_cells, neighbours, counts, source, pressure
    )
    xe, xo = swap(even, "gx", 0), swap(odd, "gx", 1)
    even, odd = middle_call(pressure, rhs, xe, xo)
    ye, yo = swap(even, "gy", 0), swap(odd, "gy", 1)
    out = sweeps_call(lax.axis_size("gx"), lax.axis_size("gy"), pressure, rhs, xe, xo, ye, yo)
    return out, kappa


def solution(mesh):
    placed = (
        P(None, "gx", "gy", None),
        P("gx", "gy", None),
        P("gx", "gy", None),
        P("gx", "gy", None, None),
        P("gx", "gy"),
        P("gx", "gy", None),
        P("gx", "gy", None),
    )
    return jax.shard_map(
        per_device,
        mesh=mesh,
        in_specs=placed,
        out_specs=(P("gx", "gy", None), P("gx", "gy", None)),
        check_vma=False,
    )
```

time: 339 us -> 35.6 us (0.11)
  the two profiles are of different devices: /device:TPU:260 before, /device:TPU:3 now
where the time goes in v1:
time: 35.6 us; the launch traced here: 35 us
  starting transfers between devices  15.1 us (42%)
  Pallas kernels  7.53 us (21%)
  local copies, waits for them, and re-layouts  5.89 us (17%)
  waiting for transfers between devices  5.09 us (14%)
  between operations  1.37 us (4%)
    ppermute x4, starting transfers between devices, swap(): return lax.ppermute(value, axis, pairs)  15.1 us
    unnamed x22, local copies, waits for them, and re-layouts  5.89 us
    ppermute x4, waiting for transfers between devices, swap(): return lax.ppermute(value, axis, pairs)  5.09 us
    pallas_call x1, Pallas kernels, curvature_call(): pl.pallas_call(curvature_kernel, out_shape=(jax.ShapeDtypeStruct((1, 1, S...  4.32 us
    pallas_call x1, Pallas kernels, sweeps_call(): pl.pallas_call(functools.partial(sweeps_kernel, n_gx, n_gy), out_shape=ja...  1.78 us
    pallas_call x1, Pallas kernels, middle_call(): pl.pallas_call(middle_kernel, out_shape=(strip, strip), in_specs=[vmem] *...  1.43 us
  transfers between devices with their start and end apart: 4, of which 2 were waited for; matrix products, arithmetic and copies ran while one was open for 0% of the time, Pallas kernels for 0%

profile of v1, /device:TPU:3, one launch (start us, length us, event | category | flops | bytes accessed | tf_op | source)
XLA Modules:
  0.0 35.0 jit_solution(16186152668103815816)
XLA Ops:
  0.6 0.0 copy-start.6
  1.3 0.0 copy-done.6
  1.3 0.0 copy-start
  1.3 0.7 %copy-done = f32[8,8,128]{2,1,0:T(8,128)S(1)} copy-done((f32[8,8,128]{2,1,0:T(8,128)S(1)}, f32[8,8,128]{2,1,0:T(8,128)}, u32[]{:S(2)}) %copy-start) | copy-done | bytes 32792
  2.1 0.0 copy-start.2
  2.1 0.9 %copy-done.2 = f32[3,8,8,128]{3,2,1,0:T(8,128)S(1)} copy-done((f32[3,8,8,128]{3,2,1,0:T(8,128)S(1)}, f32[3,8,8,128]{3,2,1,0:T(8,128)}, u32[]{:S(2)}) %copy-start.2) | copy-done | bytes 98328
  3.0 0.0 copy-start.3
  3.0 0.9 %copy-done.3 = s32[1,1,192,128]{3,2,1,0:T(8,128)S(1)} copy-done((s32[1,1,192,128]{3,2,1,0:T(8,128)S(1)}, s32[1,1,192,128]{3,2,1,0:T(8,128)}, u32[]{:S(2)}) %copy-start.3) | copy-done | bytes 98328
  3.9 0.0 copy-start.4
  3.9 0.8 %copy-done.4 = f32[8,8,128]{2,1,0:T(8,128)S(1)} copy-done((f32[8,8,128]{2,1,0:T(8,128)S(1)}, f32[8,8,128]{2,1,0:T(8,128)}, u32[]{:S(2)}) %copy-start.4) | copy-done | bytes 32792
  4.6 0.0 copy-start.5
  4.6 0.8 %copy-done.5 = f32[8,8,128]{2,1,0:T(8,128)S(1)} copy-done((f32[8,8,128]{2,1,0:T(8,128)S(1)}, f32[8,8,128]{2,1,0:T(8,128)}, u32[]{:S(2)}) %copy-start.5) | copy-done | bytes 32792
  5.4 4.3 %curvature.1 = (f32[1,1,192]{2,1,0:T(1,128)}, f32[8,8,128]{2,1,0:T(8,128)S(1)}, f32[5,8,128]{2,1,0:T(8,128)S(1)}, f32[5,8,128]{2,1,0:T(8,128)S(1)}) custom-call(f32[3,8,8,128]{3,2,1,0:T(8,128)S(1)} %copy-done.2, f32[8,8,128]{2,1,0:T(8,128)S(1)} %copy-done.4, s32[1,1,192]{2,1,0:T(1,128)S(1)} %copy-done.6, s32[1,1,192,128]{3,2,1,0:T(8,128)S(1)} %copy-done.3, ...), custom_call_target="tpu_custom_call" | custom-call | tf_op jit(solution)/shard_map/curvature/pallas_call | solution.py:161
  9.7 0.0 copy-start.1
  9.7 0.6 %copy-done.1 = f32[8,8,128]{2,1,0:T(8,128)} copy-done((f32[8,8,128]{2,1,0:T(8,128)}, f32[8,8,128]{2,1,0:T(8,128)S(1)}, u32[]{:S(2)}) %copy-start.1) | copy-done | bytes 32792
  10.3 2.6 %collective-permute-start = (f32[5,8,128]{2,1,0:T(8,128)S(1)}, f32[5,8,128]{2,1,0:T(8,128)S(1)}, u32[]{:S(2)}, u32[]{:S(2)}) collective-permute-start(f32[5,8,128]{2,1,0:T(8,128)S(1)} %get-tuple-element.9), channel_id=1, source_target_pairs={{0,4},{4,0},{8,12},{12,8},{16,20},{20,16},{24,28},{28,24},{32,36},... | collective-permute-start | bytes 61448 | tf_op jit(solution)/shard_map/ppermute | solution.py:253
  12.9 3.1 %collective-permute-start.1 = (f32[5,8,128]{2,1,0:T(8,128)S(1)}, f32[5,8,128]{2,1,0:T(8,128)S(1)}, u32[]{:S(2)}, u32[]{:S(2)}) collective-permute-start(f32[5,8,128]{2,1,0:T(8,128)S(1)} %get-tuple-element.10), channel_id=1, source_target_pairs={{4,8},{8,4},{12,16},{16,12},{20,24},{24,20},{28,32},{32,28},{36,40... | collective-permute-start | bytes 61448 | tf_op jit(solution)/shard_map/ppermute | solution.py:253
  16.0 0.0 collective-permute-done.xe_ref
  16.0 0.0 copy-start.7
  16.0 2.0 %collective-permute-done.1.xo_ref = f32[5,8,128]{2,1,0:T(8,128)S(1)} collective-permute-done((f32[5,8,128]{2,1,0:T(8,128)S(1)}, f32[5,8,128]{2,1,0:T(8,128)S(1)}, u32[]{:S(2)}, u32[]{:S(2)}) %collective-permute-start.1) | collective-permute-done | bytes 20512 | tf_op jit(solution)/shard_map/ppermute | solution.py:253
  18.0 0.0 copy-start.8
  18.0 0.0 copy-done.7
  18.0 0.6 %copy-done.8 = f32[5,8,128]{2,1,0:T(8,128)} copy-done((f32[5,8,128]{2,1,0:T(8,128)}, f32[5,8,128]{2,1,0:T(8,128)S(1)}, u32[]{:S(2)}) %copy-start.8) | copy-done | bytes 20504
  18.6 1.4 %edges.1 = (f32[12,8,128]{2,1,0:T(8,128)}, f32[12,8,128]{2,1,0:T(8,128)}) custom-call(f32[8,8,128]{2,1,0:T(8,128)} %pressure_ref.5, f32[8,8,128]{2,1,0:T(8,128)} %copy-done.1, f32[5,8,128]{2,1,0:T(8,128)} %copy-done.7, f32[5,8,128]{2,1,0:T(8,128)} %copy-done.8), custom_call_target="tpu_custom_call" | custom-call | tf_op jit(solution)/shard_map/edges/pallas_call | solution.py:199
  20.0 7.5 %collective-permute-start.2 = (f32[12,8,128]{2,1,0:T(8,128)}, f32[12,8,128]{2,1,0:T(8,128)S(1)}, u32[]{:S(2)}, u32[]{:S(2)}) collective-permute-start(f32[12,8,128]{2,1,0:T(8,128)} %get-tuple-element.11), channel_id=1, source_target_pairs={{0,1},{1,0},{2,3},{3,2},{4,5},{5,4},{6,7},{7,6},{8,9},{9,8},{10,11... | collective-permute-start | bytes 147464 | tf_op jit(solution)/shard_map/ppermute | solution.py:253
  27.5 1.9 %collective-permute-start.3 = (f32[12,8,128]{2,1,0:T(8,128)}, f32[12,8,128]{2,1,0:T(8,128)S(1)}, u32[]{:S(2)}, u32[]{:S(2)}) collective-permute-start(f32[12,8,128]{2,1,0:T(8,128)} %get-tuple-element.12), channel_id=1, source_target_pairs={{1,2},{2,1},{5,6},{6,5},{9,10},{10,9},{13,14},{14,13},{17,18},{18,... | collective-permute-start | bytes 147464 | tf_op jit(solution)/shard_map/ppermute | solution.py:253
  29.5 0.0 collective-permute-done.2.ye_ref
  29.5 0.0 copy-start.9
  29.5 3.1 %collective-permute-done.3.yo_ref = f32[12,8,128]{2,1,0:T(8,128)S(1)} collective-permute-done((f32[12,8,128]{2,1,0:T(8,128)}, f32[12,8,128]{2,1,0:T(8,128)S(1)}, u32[]{:S(2)}, u32[]{:S(2)}) %collective-permute-start.3) | collective-permute-done | bytes 49184 | tf_op jit(solution)/shard_map/ppermute | solution.py:253
  32.6 0.0 copy-done.9
  32.6 0.0 copy-start.10
  32.6 0.6 %copy-done.10 = f32[12,8,128]{2,1,0:T(8,128)} copy-done((f32[12,8,128]{2,1,0:T(8,128)}, f32[12,8,128]{2,1,0:T(8,128)S(1)}, u32[]{:S(2)}) %copy-start.10) | copy-done | bytes 49176
  33.2 1.8 %sweeps.1 = f32[8,8,128]{2,1,0:T(8,128)} custom-call(f32[8,8,128]{2,1,0:T(8,128)} %pressure_ref.5, f32[8,8,128]{2,1,0:T(8,128)} %copy-done.1, f32[5,8,128]{2,1,0:T(8,128)} %copy-done.7, f32[5,8,128]{2,1,0:T(8,128)} %copy-done.8, f32[12,8,128]{2,1,0:T(8,128)} %copy-done.9, f32[12,8,128]{2,1,0:T(8,128)} %copy-done.10), custom_call_target="tpu_custom_call" | custom-call | tf_op jit(solution)/shard_map/sweeps/pallas_call | solution.py:239
Async XLA Ops:
  0.6 0.7 %copy-start.6 = (s32[1,1,192]{2,1,0:T(1,128)S(1)}, s32[1,1,192]{2,1,0:T(1,128)}, u32[]{:S(2)}) copy-start(s32[1,1,192]{2,1,0:T(1,128)} %cells_ref.1) | copy-start | bytes 2308
  1.3 0.8 %copy-start = (f32[8,8,128]{2,1,0:T(8,128)S(1)}, f32[8,8,128]{2,1,0:T(8,128)}, u32[]{:S(2)}) copy-start(f32[8,8,128]{2,1,0:T(8,128)} %pressure_ref.5) | copy-start | bytes 98308
  2.1 0.9 %copy-start.2 = (f32[3,8,8,128]{3,2,1,0:T(8,128)S(1)}, f32[3,8,8,128]{3,2,1,0:T(8,128)}, u32[]{:S(2)}) copy-start(f32[3,8,8,128]{3,2,1,0:T(8,128)} %jitter_ref.1) | copy-start | bytes 294916
  3.0 0.9 %copy-start.3 = (s32[1,1,192,128]{3,2,1,0:T(8,128)S(1)}, s32[1,1,192,128]{3,2,1,0:T(8,128)}, u32[]{:S(2)}) copy-start(s32[1,1,192,128]{3,2,1,0:T(8,128)} %codes_ref.1) | copy-start | bytes 294916
  3.9 0.8 %copy-start.4 = (f32[8,8,128]{2,1,0:T(8,128)S(1)}, f32[8,8,128]{2,1,0:T(8,128)}, u32[]{:S(2)}) copy-start(f32[8,8,128]{2,1,0:T(8,128)} %colour_ref.1) | copy-start | bytes 98308
  4.6 0.8 %copy-start.5 = (f32[8,8,128]{2,1,0:T(8,128)S(1)}, f32[8,8,128]{2,1,0:T(8,128)}, u32[]{:S(2)}) copy-start(f32[8,8,128]{2,1,0:T(8,128)} %source_ref.1) | copy-start | bytes 98308
  9.7 0.6 %copy-start.1 = (f32[8,8,128]{2,1,0:T(8,128)}, f32[8,8,128]{2,1,0:T(8,128)S(1)}, u32[]{:S(2)}) copy-start(f32[8,8,128]{2,1,0:T(8,128)S(1)} %get-tuple-element.8.rhs_ref) | copy-start | bytes 98308
  10.3 5.7 %collective-permute-start = (f32[5,8,128]{2,1,0:T(8,128)S(1)}, f32[5,8,128]{2,1,0:T(8,128)S(1)}, u32[]{:S(2)}, u32[]{:S(2)}) collective-permute-start(f32[5,8,128]{2,1,0:T(8,128)S(1)} %get-tuple-element.9), channel_id=1, source_target_pairs={{0,4},{4,0},{8,12},{12,8},{16,20},{20,16},{24,28},{28,24},{32,36},... | collective-permute-start | bytes 61448 | tf_op jit(solution)/shard_map/ppermute | solution.py:253
  12.9 5.1 %collective-permute-start.1 = (f32[5,8,128]{2,1,0:T(8,128)S(1)}, f32[5,8,128]{2,1,0:T(8,128)S(1)}, u32[]{:S(2)}, u32[]{:S(2)}) collective-permute-start(f32[5,8,128]{2,1,0:T(8,128)S(1)} %get-tuple-element.10), channel_id=1, source_target_pairs={{4,8},{8,4},{12,16},{16,12},{20,24},{24,20},{28,32},{32,28},{36,40... | collective-permute-start | bytes 61448 | tf_op jit(solution)/shard_map/ppermute | solution.py:253
  16.0 2.0 %copy-start.7 = (f32[5,8,128]{2,1,0:T(8,128)}, f32[5,8,128]{2,1,0:T(8,128)S(1)}, u32[]{:S(2)}) copy-start(f32[5,8,128]{2,1,0:T(8,128)S(1)} %collective-permute-done.xe_ref) | copy-start | bytes 61444
  18.0 0.6 %copy-start.8 = (f32[5,8,128]{2,1,0:T(8,128)}, f32[5,8,128]{2,1,0:T(8,128)S(1)}, u32[]{:S(2)}) copy-start(f32[5,8,128]{2,1,0:T(8,128)S(1)} %collective-permute-done.1.xo_ref) | copy-start | bytes 61444
  20.0 9.5 %collective-permute-start.2 = (f32[12,8,128]{2,1,0:T(8,128)}, f32[12,8,128]{2,1,0:T(8,128)S(1)}, u32[]{:S(2)}, u32[]{:S(2)}) collective-permute-start(f32[12,8,128]{2,1,0:T(8,128)} %get-tuple-element.11), channel_id=1, source_target_pairs={{0,1},{1,0},{2,3},{3,2},{4,5},{5,4},{6,7},{7,6},{8,9},{9,8},{10,11... | collective-permute-start | bytes 147464 | tf_op jit(solution)/shard_map/ppermute | solution.py:253
  27.5 5.0 %collective-permute-start.3 = (f32[12,8,128]{2,1,0:T(8,128)}, f32[12,8,128]{2,1,0:T(8,128)S(1)}, u32[]{:S(2)}, u32[]{:S(2)}) collective-permute-start(f32[12,8,128]{2,1,0:T(8,128)} %get-tuple-element.12), channel_id=1, source_target_pairs={{1,2},{2,1},{5,6},{6,5},{9,10},{10,9},{13,14},{14,13},{17,18},{18,... | collective-permute-start | bytes 147464 | tf_op jit(solution)/shard_map/ppermute | solution.py:253
  29.5 3.1 %copy-start.9 = (f32[12,8,128]{2,1,0:T(8,128)}, f32[12,8,128]{2,1,0:T(8,128)S(1)}, u32[]{:S(2)}) copy-start(f32[12,8,128]{2,1,0:T(8,128)S(1)} %collective-permute-done.2.ye_ref) | copy-start | bytes 147460
  32.6 0.6 %copy-start.10 = (f32[12,8,128]{2,1,0:T(8,128)}, f32[12,8,128]{2,1,0:T(8,128)S(1)}, u32[]{:S(2)}) copy-start(f32[12,8,128]{2,1,0:T(8,128)S(1)} %collective-permute-done.3.yo_ref) | copy-start | bytes 147460

commit v2 on v1

--- a/solution.py
+++ b/solution.py
@@ -43,19 +43,26 @@
 
 
 def curvature_kernel(
-    jitter_ref, colour_ref, cells_ref, codes_ref, counts_ref, source_ref, pressure_ref,
-    kappa_ref, rhs_ref, even_ref, odd_ref,
+    jitter_hbm, colour_hbm, cells_hbm, codes_hbm, counts_ref, source_hbm, pressure_hbm,
+    kappa_ref, own_ref, rhs_ref, even_ref, odd_ref,
+    jitter_ref, colour_ref, cells_ref, codes_ref, source_ref, arrived,
     table, hot, window, place, row, moments,
 ):
-    zero = jnp.zeros((ROWS, LANES), jnp.bfloat16)
-    for c in range(4):
-        value = colour_ref[...] if c == 3 else jitter_ref[c]
-        for q, piece in enumerate(pieces(value.reshape(ROWS, LANES))):
-            for p in range(2):
-                rows = pl.ds(c * LANES + p * ROWS, ROWS)
-                table[q, rows, p * LANES : (p + 1) * LANES] = piece
-                table[q, rows, (1 - p) * LANES : (2 - p) * LANES] = zero
-
+    copies = [
+        pltpu.make_async_copy(source, target, arrived.at[i])
+        for i, (source, target) in enumerate((
+            (cells_hbm, cells_ref),
+            (jitter_hbm, jitter_ref),
+            (colour_hbm, colour_ref),
+            (codes_hbm, codes_ref),
+            (source_hbm, source_ref),
+            (pressure_hbm, own_ref),
+        ))
+    ]
+    for copy in copies:
+        copy.start()
+
+    copies[0].wait()
     row[...] = jnp.zeros_like(row)
     row[0:1, 0:SLOTS] = cells_ref[0]
     cells_row = row[0:1, :]
@@ -74,6 +81,17 @@
         hot[d * SLOTS : (d + 1) * SLOTS, p * LANES : (p + 1) * LANES] = jnp.where(
             lane == target, 1.0, 0.0
         ).astype(jnp.bfloat16)
+
+    copies[1].wait()
+    copies[2].wait()
+    zero = jnp.zeros((ROWS, LANES), jnp.bfloat16)
+    for c in range(4):
+        value = colour_ref[...] if c == 3 else jitter_ref[c]
+        for q, piece in enumerate(pieces(value.reshape(ROWS, LANES))):
+            for p in range(2):
+                rows = pl.ds(c * LANES + p * ROWS, ROWS)
+                table[q, rows, p * LANES : (p + 1) * LANES] = piece
+                table[q, rows, (1 - p) * LANES : (2 - p) * LANES] = zero
 
     contract = (((1,), (1,)), ((), ()))
     acc = lax.dot_general(hot[...], table[0], contract, preferred_element_type=jnp.float32)
@@ -122,11 +140,14 @@
         return carry
 
     moments[SLOTS:, :] = jnp.zeros((2 * LANES - SLOTS, LANES), jnp.float32)
+    copies[3].wait()
     lax.fori_loop(0, SLOTS // STEP, group, 0)
 
     sums = jnp.concatenate([moments[0:LANES, :].T, moments[LANES:, :].T], axis=1)
     kappa = final_curvature(*[sums[q : q + 1, :] for q in range(10)])
     slot = lax.broadcasted_iota(jnp.int32, (1, 2 * LANES), 1)
+    for copy in copies[4:]:
+        copy.wait()
     kappa = jnp.where(slot < counts_ref[0, 0], kappa, 0.0)
     kappa_ref[0] = kappa[:, :SLOTS]
 
@@ -143,7 +164,7 @@
     rhs = source_ref[...] + added.reshape(8, 8, LANES)
     rhs_ref[...] = rhs
     even = lax.rem(lax.axis_index("gx"), 2) == 0
-    pressure = pressure_ref[...]
+    pressure = own_ref[...]
 
     def send(ref, high):
         ref[0:3] = jnp.where(high, pressure[5:8], pressure[0:3])
@@ -153,17 +174,24 @@
     send(odd_ref, jnp.logical_not(even))
 
 
-def curvature_call(jitter, colour, cells, codes, counts, source, pressure):
+def curvature_call(*values):
     tile = jax.ShapeDtypeStruct((8, 8, LANES), jnp.float32)
     slab = jax.ShapeDtypeStruct((5, 8, LANES), jnp.float32)
     vmem = pl.BlockSpec(memory_space=pltpu.VMEM)
+    hbm = pl.BlockSpec(memory_space=pltpu.HBM)
     smem = pl.BlockSpec(memory_space=pltpu.SMEM)
     return pl.pallas_call(
         curvature_kernel,
-        out_shape=(jax.ShapeDtypeStruct((1, 1, SLOTS), jnp.float32), tile, slab, slab),
-        in_specs=[vmem, vmem, vmem, vmem, smem, vmem, vmem],
-        out_specs=(vmem, vmem, vmem, vmem),
+        out_shape=(jax.ShapeDtypeStruct((1, 1, SLOTS), jnp.float32), tile, tile, slab, slab),
+        in_specs=[hbm] * 4 + [smem] + [hbm] * 2,
+        out_specs=(vmem,) * 5,
         scratch_shapes=[
+            pltpu.VMEM((3, 8, 8, LANES), jnp.float32),
+            pltpu.VMEM((8, 8, LANES), jnp.float32),
+            pltpu.VMEM((1, 1, SLOTS), jnp.int32),
+            pltpu.VMEM((1, 1, SLOTS, LANES), jnp.int32),
+            pltpu.VMEM((8, 8, LANES), jnp.float32),
+            pltpu.SemaphoreType.DMA((6,)),
             pltpu.VMEM((3, 4 * LANES, 2 * LANES), jnp.bfloat16),
             pltpu.VMEM((4 * SLOTS, 2 * LANES), jnp.bfloat16),
             pltpu.VMEM((4 * SLOTS, 4 * LANES), jnp.float32),
@@ -171,9 +199,9 @@
             pltpu.VMEM((8, 2 * LANES), jnp.int32),
             pltpu.VMEM((2 * LANES, LANES), jnp.float32),
         ],
-        compiler_params=pltpu.CompilerParams(vmem_limit_bytes=32 * 2**20),
+        compiler_params=pltpu.CompilerParams(vmem_limit_bytes=16 * 2**20),
         name="curvature",
-    )(jitter, colour, cells, codes, counts, source, pressure)
+    )(*values)
 
 
 def sides(first, second, even):
@@ -181,9 +209,9 @@
 
 
 def middle_kernel(pressure_ref, rhs_ref, xe_ref, xo_ref, even_ref, odd_ref):
-    even_x = lax.rem(lax.axis_index("gx"), 2) == 0
+    odd_x = lax.rem(lax.axis_index("gx"), 2)
     even_y = lax.rem(lax.axis_index("gy"), 2) == 0
-    below, above = sides(xe_ref[...], xo_ref[...], even_x)
+    below, above = sides(xe_ref[1 - odd_x], xo_ref[...], odd_x == 0)
     planes = jnp.concatenate([below[1:3], pressure_ref[...], above[0:2]], axis=0)
     rhs = jnp.concatenate([below[3:5], rhs_ref[...], above[3:5]], axis=0)
     sub = lax.broadcasted_iota(jnp.int32, (1, 8, LANES), 1)
@@ -201,14 +229,20 @@
         out_shape=(strip, strip),
         in_specs=[vmem] * 4,
         out_specs=(vmem, vmem),
+        compiler_params=pltpu.CompilerParams(vmem_limit_bytes=8 * 2**20),
         name="edges",
     )(pressure, rhs, xe, xo)
 
 
-def sweeps_kernel(n_gx, n_gy, pressure_ref, rhs_ref, xe_ref, xo_ref, ye_ref, yo_ref, out_ref):
+def sweeps_kernel(
+    n_gx, n_gy, kappa_ref, pressure_ref, rhs_ref, xe_ref, xo_ref, ye_ref, yo_ref,
+    out_ref, curvature_ref,
+):
     at_x, at_y = lax.axis_index("gx"), lax.axis_index("gy")
-    below, above = sides(xe_ref[...], xo_ref[...], lax.rem(at_x, 2) == 0)
-    left, right = sides(ye_ref[...], yo_ref[...], lax.rem(at_y, 2) == 0)
+    odd_x, odd_y = lax.rem(at_x, 2), lax.rem(at_y, 2)
+    below, above = sides(xe_ref[1 - odd_x], xo_ref[...], odd_x == 0)
+    left, right = sides(ye_ref[1 - odd_y], yo_ref[...], odd_y == 0)
+    curvature_ref[...] = kappa_ref[...]
     own = jnp.concatenate([below[0:3], pressure_ref[...], above[0:3]], axis=0)
     rhs = jnp.concatenate([below[3:5], rhs_ref[...], above[3:5]], axis=0)
     nothing = jnp.zeros((1, 8, LANES), jnp.float32)
@@ -238,30 +272,44 @@
     vmem = pl.BlockSpec(memory_space=pltpu.VMEM)
     return pl.pallas_call(
         functools.partial(sweeps_kernel, n_gx, n_gy),
-        out_shape=jax.ShapeDtypeStruct((8, 8, LANES), jnp.float32),
-        in_specs=[vmem] * 6,
-        out_specs=vmem,
+        out_shape=(
+            jax.ShapeDtypeStruct((8, 8, LANES), jnp.float32),
+            jax.ShapeDtypeStruct((1, 1, SLOTS), jnp.float32),
+        ),
+        in_specs=[vmem] * 7,
+        out_specs=(vmem, vmem),
+        compiler_params=pltpu.CompilerParams(vmem_limit_bytes=8 * 2**20),
         name="sweeps",
     )(*values)
 
 
-def swap(value, axis, odd):
-    size = lax.axis_size(axis)
+def swap_odd(value, axis):
     pairs = []
-    for i in range(odd, size - 1, 2):
+    for i in range(1, lax.axis_size(axis) - 1, 2):
         pairs += [(i, i + 1), (i + 1, i)]
     return lax.ppermute(value, axis, pairs)
 
 
+def gather_even(value, axis):
+    groups = [[i, i + 1] for i in range(0, lax.axis_size(axis), 2)]
+    return lax.all_gather(value, axis, axis=0, axis_index_groups=groups)
+
+
+def held(value):
+    return pltpu.with_memory_space_constraint(value, pltpu.HBM)
+
+
 def per_device(jitter, colour, surface_cells, neighbours, counts, pressure, source):
-    kappa, rhs, even, odd = curvature_call(
-        jitter, colour, surface_cells, neighbours, counts, source, pressure
+    kappa, own, rhs, even, odd = curvature_call(
+        held(jitter), held(colour), held(surface_cells), held(neighbours),
+        counts, held(source), held(pressure),
     )
-    xe, xo = swap(even, "gx", 0), swap(odd, "gx", 1)
-    even, odd = middle_call(pressure, rhs, xe, xo)
-    ye, yo = swap(even, "gy", 0), swap(odd, "gy", 1)
-    out = sweeps_call(lax.axis_size("gx"), lax.axis_size("gy"), pressure, rhs, xe, xo, ye, yo)
-    return out, kappa
+    xo, xe = swap_odd(odd, "gx"), gather_even(even, "gx")
+    even, odd = middle_call(own, rhs, xe, xo)
+    yo, ye = swap_odd(odd, "gy"), gather_even(even, "gy")
+    return sweeps_call(
+        lax.axis_size("gx"), lax.axis_size("gy"), kappa, own, rhs, xe, xo, ye, yo
+    )
 
 
 def solution(mesh):

time: 35.6 us -> 23.8 us (0.67)
  the two profiles are of different devices: /device:TPU:3 before, /device:TPU:258 now
where the time goes in v2:
time: 23.8 us; the launch traced here: 23.6 us
  starting transfers between devices  7.3 us (31%)
  blocking collectives  6.6 us (28%)
  Pallas kernels  5.76 us (24%)
  waiting for transfers between devices  2.67 us (11%)
  between operations  1.31 us (6%)
    ppermute x2, starting transfers between devices, swap_odd(): return lax.ppermute(value, axis, pairs)  7.3 us
    all_gather x2, blocking collectives, gather_even(): return lax.all_gather(value, axis, axis=0, axis_index_groups=groups)  6.6 us
    pallas_call x1, Pallas kernels, curvature_call(): pl.pallas_call(curvature_kernel, out_shape=(jax.ShapeDtypeStruct((1, 1, S...  4.85 us
    ppermute x2, waiting for transfers between devices, swap_odd(): return lax.ppermute(value, axis, pairs)  2.67 us
    pallas_call x1, Pallas kernels, sweeps_call(): pl.pallas_call(functools.partial(sweeps_kernel, n_gx, n_gy), out_shape=(j...  0.89 us
  transfers between devices with their start and end apart: 2, of which 1 were waited for; matrix products, arithmetic and copies ran while one was open for 0% of the time, Pallas kernels for 0%

profile of v2, /device:TPU:258, one launch (start us, length us, event | category | flops | bytes accessed | tf_op | source)
XLA Modules:
  0.0 23.6 jit_solution(2104761222289377920)
XLA Ops:
  1.3 4.9 %curvature.1 = (f32[1,1,192]{2,1,0:T(1,128)S(1)}, f32[8,8,128]{2,1,0:T(8,128)S(1)}, f32[8,8,128]{2,1,0:T(8,128)S(1)}, f32[5,8,128]{2,1,0:T(8,128)S(1)}, f32[5,8,128]{2,1,0:T(8,128)S(1)}) custom-call(f32[3,8,8,128]{3,2,1,0:T(8,128)} %jitter_hbm.1, f32[8,8,128]{2,1,0:T(8,128)} %colour_hbm.1, s32[1,1,192]{2,1,0:T(1,128)} %cells_hbm.1, ...), custom_call_target="tpu_custom_call" | custom-call | tf_op jit(solution)/shard_map/curvature/pallas_call | solution.py:183
  6.1 3.9 %collective-permute-start = (f32[5,8,128]{2,1,0:T(8,128)S(1)}, f32[5,8,128]{2,1,0:T(8,128)S(1)}, u32[]{:S(2)}, u32[]{:S(2)}) collective-permute-start(f32[5,8,128]{2,1,0:T(8,128)S(1)} %get-tuple-element.13), channel_id=1, source_target_pairs={{4,8},{8,4},{12,16},{16,12},{20,24},{24,20},{28,32},{32,28},{36,40... | collective-permute-start | bytes 61448 | tf_op jit(solution)/shard_map/ppermute | solution.py:290
  10.0 1.8 %all-gather = f32[10,8,128]{2,1,0:T(8,128)S(1)} all-gather(f32[5,8,128]{2,1,0:T(8,128)S(1)} %get-tuple-element.12), channel_id=2, replica_groups={{0,4},{8,12},{16,20},{24,28},{32,36},{40,44},{48,52},{56,60},{64,68},{7..., dimensions={0}, use_global_device_ids=true | all-gather | bytes 61440 | tf_op jit(solution)/shard_map/all_gather | solution.py:295
  11.9 2.7 %collective-permute-done.xo_ref = f32[5,8,128]{2,1,0:T(8,128)S(1)} collective-permute-done((f32[5,8,128]{2,1,0:T(8,128)S(1)}, f32[5,8,128]{2,1,0:T(8,128)S(1)}, u32[]{:S(2)}, u32[]{:S(2)}) %collective-permute-start) | collective-permute-done | bytes 20512 | tf_op jit(solution)/shard_map/ppermute | solution.py:290
  14.6 3.4 %collective-permute-start.1 = (f32[12,8,128]{2,1,0:T(8,128)S(1)}, f32[12,8,128]{2,1,0:T(8,128)S(1)}, u32[]{:S(2)}, u32[]{:S(2)}) collective-permute-start(f32[12,8,128]{2,1,0:T(8,128)S(1)} %get-tuple-element.15), channel_id=1, source_target_pairs={{1,2},{2,1},{5,6},{6,5},{9,10},{10,9},{13,14},{14,13},{17,18},{18,... | collective-permute-start | bytes 147464 | tf_op jit(solution)/shard_map/ppermute | solution.py:290
  18.0 4.8 %all-gather.1 = f32[24,8,128]{2,1,0:T(8,128)S(1)} all-gather(f32[12,8,128]{2,1,0:T(8,128)S(1)} %get-tuple-element.14), channel_id=3, replica_groups={{0,1},{2,3},{4,5},{6,7},{8,9},{10,11},{12,13},{14,15},{16,17},{18,19},{..., dimensions={0}, use_global_device_ids=true | all-gather | bytes 147456 | tf_op jit(solution)/shard_map/all_gather | solution.py:295
  22.8 0.0 collective-permute-done.1.yo_ref
  22.8 0.9 %sweeps.1 = (f32[8,8,128]{2,1,0:T(8,128)}, f32[1,1,192]{2,1,0:T(1,128)}) custom-call(f32[1,1,192]{2,1,0:T(1,128)S(1)} %get-tuple-element.9.kappa_ref, f32[8,8,128]{2,1,0:T(8,128)S(1)} %get-tuple-element.10.pressure_ref, f32[8,8,128]{2,1,0:T(8,128)S(1)} %get-tuple-element.11.rhs_ref, f32[2,5,8,128]{3,2,1,0:T(8,128)S(1)} %bitcast.4, ...), custom_call_target="tpu_custom_call" | custom-call | tf_op jit(solution)/shard_map/sweeps/pallas_call | solution.py:273
  (1 shorter events, 0.0 us)
Async XLA Ops:
  6.1 8.4 %collective-permute-start = (f32[5,8,128]{2,1,0:T(8,128)S(1)}, f32[5,8,128]{2,1,0:T(8,128)S(1)}, u32[]{:S(2)}, u32[]{:S(2)}) collective-permute-start(f32[5,8,128]{2,1,0:T(8,128)S(1)} %get-tuple-element.13), channel_id=1, source_target_pairs={{4,8},{8,4},{12,16},{16,12},{20,24},{24,20},{28,32},{32,28},{36,40... | collective-permute-start | bytes 61448 | tf_op jit(solution)/shard_map/ppermute | solution.py:290
  14.6 8.2 %collective-permute-start.1 = (f32[12,8,128]{2,1,0:T(8,128)S(1)}, f32[12,8,128]{2,1,0:T(8,128)S(1)}, u32[]{:S(2)}, u32[]{:S(2)}) collective-permute-start(f32[12,8,128]{2,1,0:T(8,128)S(1)} %get-tuple-element.15), channel_id=1, source_target_pairs={{1,2},{2,1},{5,6},{6,5},{9,10},{10,9},{13,14},{14,13},{17,18},{18,... | collective-permute-start | bytes 147464 | tf_op jit(solution)/shard_map/ppermute | solution.py:290

commit v3 on v2

--- a/solution.py
+++ b/solution.py
@@ -12,7 +12,7 @@
 SLOTS = 192
 LANES = 128
 ROWS = 64
-STEP = 24
+STEP = 192
 
 
 def pieces(value):
@@ -75,29 +75,26 @@
 
     lane = lax.broadcasted_iota(jnp.int32, (SLOTS, LANES), 1)
     z_of = place[...] & 127
-    for step in range(8):
+    for step in range(7):
         target = jnp.clip(z_of + (step - 3), 0, LANES - 1)
-        d, p = step // 2, step % 2
-        hot[d * SLOTS : (d + 1) * SLOTS, p * LANES : (p + 1) * LANES] = jnp.where(
-            lane == target, 1.0, 0.0
-        ).astype(jnp.bfloat16)
+        one = jnp.where(lane == target, 1.0, 0.0).astype(jnp.bfloat16)
+        for q in range(3):
+            hot[step % 2, (step // 2) * SLOTS : (step // 2 + 1) * SLOTS, q * LANES : (q + 1) * LANES] = one
 
     copies[1].wait()
     copies[2].wait()
-    zero = jnp.zeros((ROWS, LANES), jnp.bfloat16)
     for c in range(4):
         value = colour_ref[...] if c == 3 else jitter_ref[c]
         for q, piece in enumerate(pieces(value.reshape(ROWS, LANES))):
-            for p in range(2):
-                rows = pl.ds(c * LANES + p * ROWS, ROWS)
-                table[q, rows, p * LANES : (p + 1) * LANES] = piece
-                table[q, rows, (1 - p) * LANES : (2 - p) * LANES] = zero
+            columns = slice(q * LANES, (q + 1) * LANES)
+            table[0, c * ROWS : (c + 1) * ROWS, columns] = piece
+            table[1, (c ^ 1) * ROWS : ((c ^ 1) + 1) * ROWS, columns] = piece
 
     contract = (((1,), (1,)), ((), ()))
-    acc = lax.dot_general(hot[...], table[0], contract, preferred_element_type=jnp.float32)
-    acc = acc + lax.dot_general(hot[...], table[1], contract, preferred_element_type=jnp.float32)
-    acc = acc + lax.dot_general(hot[...], table[2], contract, preferred_element_type=jnp.float32)
-    window[...] = acc
+    window[0] = lax.dot_general(hot[0], table[0], contract, preferred_element_type=jnp.float32)
+    window[1, : 3 * SLOTS] = lax.dot_general(
+        hot[1, : 3 * SLOTS], table[1], contract, preferred_element_type=jnp.float32
+    )
 
     lane_step = lax.broadcasted_iota(jnp.int32, (STEP, LANES), 1)
 
@@ -114,19 +111,29 @@
         near_x = jnp.clip(x + a - 3, 0, 7)
         near_y = jnp.clip(y + b - 3, 0, 7)
         near_z = jnp.clip(z + dz - 3, 0, LANES - 1)
-        index = (dz & 1) * ROWS + near_x * 8 + near_y
-        centre = ROWS + (cell >> 7)
+        near = near_x * 8 + near_y
+        index = (near + (dz & 1) * ROWS, near + (1 - (dz & 1)) * ROWS)
+        own = cell >> 7
+        centre = (own + ROWS, own)
         d = dz >> 1
         low, first, third = d < 2, d < 1, d < 3
+        left = lane_step < ROWS
+        tabs = []
+        for k in range(4):
+            at = pl.ds(pl.multiple_of(k * SLOTS + start, 8), STEP)
+            for pair in range(2):
+                cols = slice(pair * LANES, (pair + 1) * LANES)
+                even = window[0, at, cols]
+                odd = window[1, at, cols] if k < 3 else even
+                tabs.append((jnp.where(left, even, odd), jnp.where(left, odd, even)))
         diff = []
         for c in range(4):
-            cols = slice(c * LANES, (c + 1) * LANES)
-            tabs = [window[pl.ds(pl.multiple_of(k * SLOTS + start, 8), STEP), cols] for k in range(4)]
-            got = [lane_take(t, index) for t in tabs]
+            mine = [tabs[2 * k + c // 2][c % 2] for k in range(4)]
+            got = [lane_take(t, index[c % 2]) for t in mine]
             value = jnp.where(
                 low, jnp.where(first, got[0], got[1]), jnp.where(third, got[2], got[3])
             )
-            diff.append(value - lane_take(tabs[1], centre))
+            diff.append(value - lane_take(mine[1], centre[c % 2]))
         ox = (near_x - x).astype(jnp.float32) + diff[0]
         oy = (near_y - y).astype(jnp.float32) + diff[1]
         oz = (near_z - z).astype(jnp.float32) + diff[2]
@@ -156,10 +163,10 @@
     added = jnp.zeros((ROWS, LANES), jnp.float32)
     for piece in pieces(spread):
         added = added + jnp.dot(
-            piece[:, :LANES], hot[SLOTS : SLOTS + LANES, LANES:], preferred_element_type=jnp.float32
+            piece[:, :LANES], hot[1, SLOTS : SLOTS + LANES, :LANES], preferred_element_type=jnp.float32
         )
         added = added + jnp.dot(
-            piece[:, LANES:SLOTS], hot[SLOTS + LANES : 2 * SLOTS, LANES:], preferred_element_type=jnp.float32
+            piece[:, LANES:SLOTS], hot[1, SLOTS + LANES : 2 * SLOTS, :LANES], preferred_element_type=jnp.float32
         )
     rhs = source_ref[...] + added.reshape(8, 8, LANES)
     rhs_ref[...] = rhs
@@ -192,9 +199,9 @@
             pltpu.VMEM((1, 1, SLOTS, LANES), jnp.int32),
             pltpu.VMEM((8, 8, LANES), jnp.float32),
             pltpu.SemaphoreType.DMA((6,)),
-            pltpu.VMEM((3, 4 * LANES, 2 * LANES), jnp.bfloat16),
-            pltpu.VMEM((4 * SLOTS, 2 * LANES), jnp.bfloat16),
-            pltpu.VMEM((4 * SLOTS, 4 * LANES), jnp.float32),
+            pltpu.VMEM((2, 4 * ROWS, 3 * LANES), jnp.bfloat16),
+            pltpu.VMEM((2, 4 * SLOTS, 3 * LANES), jnp.bfloat16),
+            pltpu.VMEM((2, 4 * SLOTS, 4 * ROWS), jnp.float32),
             pltpu.VMEM((SLOTS, LANES), jnp.int32),
             pltpu.VMEM((8, 2 * LANES), jnp.int32),
             pltpu.VMEM((2 * LANES, LANES), jnp.float32),

time: 23.8 us -> 22.7 us (0.954)
  Pallas kernels: 5.76 us -> 4.63 us
    pallas_call x1, Pallas kernels: 4.85 us -> 3.73 us  [curvature_call(): pl.pallas_call(curvature_kernel, out_shape=(jax.ShapeDtypeStruct((1, 1, S...]
where the time goes in v3:
time: 22.7 us; the launch traced here: 22.5 us
  starting transfers between devices  7.31 us (32%)
  blocking collectives  6.6 us (29%)
  Pallas kernels  4.63 us (20%)
  waiting for transfers between devices  2.67 us (12%)
  between operations  1.31 us (6%)
    ppermute x2, starting transfers between devices, swap_odd(): return lax.ppermute(value, axis, pairs)  7.31 us
    all_gather x2, blocking collectives, gather_even(): return lax.all_gather(value, axis, axis=0, axis_index_groups=groups)  6.6 us
    pallas_call x1, Pallas kernels, curvature_call(): pl.pallas_call(curvature_kernel, out_shape=(jax.ShapeDtypeStruct((1, 1, S...  3.73 us
    ppermute x2, waiting for transfers between devices, swap_odd(): return lax.ppermute(value, axis, pairs)  2.67 us
    pallas_call x1, Pallas kernels, sweeps_call(): pl.pallas_call(functools.partial(sweeps_kernel, n_gx, n_gy), out_shape=(j...  0.89 us
  transfers between devices with their start and end apart: 2, of which 1 were waited for; matrix products, arithmetic and copies ran while one was open for 0% of the time, Pallas kernels for 0%

profile of v3, /device:TPU:258, one launch (start us, length us, event | category | flops | bytes accessed | tf_op | source)
XLA Modules:
  0.0 22.5 jit_solution(18018688835890292695)
XLA Ops:
  1.3 3.7 %curvature.1 = (f32[1,1,192]{2,1,0:T(1,128)S(1)}, f32[8,8,128]{2,1,0:T(8,128)S(1)}, f32[8,8,128]{2,1,0:T(8,128)S(1)}, f32[5,8,128]{2,1,0:T(8,128)S(1)}, f32[5,8,128]{2,1,0:T(8,128)S(1)}) custom-call(f32[3,8,8,128]{3,2,1,0:T(8,128)} %jitter_hbm.1, f32[8,8,128]{2,1,0:T(8,128)} %colour_hbm.1, s32[1,1,192]{2,1,0:T(1,128)} %cells_hbm.1, ...), custom_call_target="tpu_custom_call" | custom-call | tf_op jit(solution)/shard_map/curvature/pallas_call | solution.py:190
  5.0 3.9 %collective-permute-start = (f32[5,8,128]{2,1,0:T(8,128)S(1)}, f32[5,8,128]{2,1,0:T(8,128)S(1)}, u32[]{:S(2)}, u32[]{:S(2)}) collective-permute-start(f32[5,8,128]{2,1,0:T(8,128)S(1)} %get-tuple-element.13), channel_id=1, source_target_pairs={{4,8},{8,4},{12,16},{16,12},{20,24},{24,20},{28,32},{32,28},{36,40... | collective-permute-start | bytes 61448 | tf_op jit(solution)/shard_map/ppermute | solution.py:297
  8.9 1.8 %all-gather = f32[10,8,128]{2,1,0:T(8,128)S(1)} all-gather(f32[5,8,128]{2,1,0:T(8,128)S(1)} %get-tuple-element.12), channel_id=2, replica_groups={{0,4},{8,12},{16,20},{24,28},{32,36},{40,44},{48,52},{56,60},{64,68},{7..., dimensions={0}, use_global_device_ids=true | all-gather | bytes 61440 | tf_op jit(solution)/shard_map/all_gather | solution.py:302
  10.8 2.7 %collective-permute-done.xo_ref = f32[5,8,128]{2,1,0:T(8,128)S(1)} collective-permute-done((f32[5,8,128]{2,1,0:T(8,128)S(1)}, f32[5,8,128]{2,1,0:T(8,128)S(1)}, u32[]{:S(2)}, u32[]{:S(2)}) %collective-permute-start) | collective-permute-done | bytes 20512 | tf_op jit(solution)/shard_map/ppermute | solution.py:297
  13.5 3.4 %collective-permute-start.1 = (f32[12,8,128]{2,1,0:T(8,128)S(1)}, f32[12,8,128]{2,1,0:T(8,128)S(1)}, u32[]{:S(2)}, u32[]{:S(2)}) collective-permute-start(f32[12,8,128]{2,1,0:T(8,128)S(1)} %get-tuple-element.15), channel_id=1, source_target_pairs={{1,2},{2,1},{5,6},{6,5},{9,10},{10,9},{13,14},{14,13},{17,18},{18,... | collective-permute-start | bytes 147464 | tf_op jit(solution)/shard_map/ppermute | solution.py:297
  16.9 4.8 %all-gather.1 = f32[24,8,128]{2,1,0:T(8,128)S(1)} all-gather(f32[12,8,128]{2,1,0:T(8,128)S(1)} %get-tuple-element.14), channel_id=3, replica_groups={{0,1},{2,3},{4,5},{6,7},{8,9},{10,11},{12,13},{14,15},{16,17},{18,19},{..., dimensions={0}, use_global_device_ids=true | all-gather | bytes 147456 | tf_op jit(solution)/shard_map/all_gather | solution.py:302
  21.6 0.0 collective-permute-done.1.yo_ref
  21.6 0.9 %sweeps.1 = (f32[8,8,128]{2,1,0:T(8,128)}, f32[1,1,192]{2,1,0:T(1,128)}) custom-call(f32[1,1,192]{2,1,0:T(1,128)S(1)} %get-tuple-element.9.kappa_ref, f32[8,8,128]{2,1,0:T(8,128)S(1)} %get-tuple-element.10.pressure_ref, f32[8,8,128]{2,1,0:T(8,128)S(1)} %get-tuple-element.11.rhs_ref, f32[2,5,8,128]{3,2,1,0:T(8,128)S(1)} %bitcast.4, ...), custom_call_target="tpu_custom_call" | custom-call | tf_op jit(solution)/shard_map/sweeps/pallas_call | solution.py:280
  (1 shorter events, 0.0 us)
Async XLA Ops:
  5.0 8.4 %collective-permute-start = (f32[5,8,128]{2,1,0:T(8,128)S(1)}, f32[5,8,128]{2,1,0:T(8,128)S(1)}, u32[]{:S(2)}, u32[]{:S(2)}) collective-permute-start(f32[5,8,128]{2,1,0:T(8,128)S(1)} %get-tuple-element.13), channel_id=1, source_target_pairs={{4,8},{8,4},{12,16},{16,12},{20,24},{24,20},{28,32},{32,28},{36,40... | collective-permute-start | bytes 61448 | tf_op jit(solution)/shard_map/ppermute | solution.py:297
  13.5 8.2 %collective-permute-start.1 = (f32[12,8,128]{2,1,0:T(8,128)S(1)}, f32[12,8,128]{2,1,0:T(8,128)S(1)}, u32[]{:S(2)}, u32[]{:S(2)}) collective-permute-start(f32[12,8,128]{2,1,0:T(8,128)S(1)} %get-tuple-element.15), channel_id=1, source_target_pairs={{1,2},{2,1},{5,6},{6,5},{9,10},{10,9},{13,14},{14,13},{17,18},{18,... | collective-permute-start | bytes 147464 | tf_op jit(solution)/shard_map/ppermute | solution.py:297

commit v4 on v3

--- a/solution.py
+++ b/solution.py
@@ -13,6 +13,7 @@
 LANES = 128
 ROWS = 64
 STEP = 192
+SCALE = 32767.0 / 0.3
 
 
 def pieces(value):
@@ -81,10 +82,11 @@
         for q in range(3):
             hot[step % 2, (step // 2) * SLOTS : (step // 2 + 1) * SLOTS, q * LANES : (q + 1) * LANES] = one
 
-    copies[1].wait()
-    copies[2].wait()
-    for c in range(4):
-        value = colour_ref[...] if c == 3 else jitter_ref[c]
+    for copy in copies[1:]:
+        copy.wait()
+    whole_x = jnp.round(jitter_ref[0] * SCALE)
+    whole_y = jnp.round(jitter_ref[1] * SCALE) + 32768.0
+    for c, value in enumerate((whole_x, jitter_ref[2], whole_y, colour_ref[...])):
         for q, piece in enumerate(pieces(value.reshape(ROWS, LANES))):
             columns = slice(q * LANES, (q + 1) * LANES)
             table[0, c * ROWS : (c + 1) * ROWS, columns] = piece
@@ -99,7 +101,7 @@
     lane_step = lax.broadcasted_iota(jnp.int32, (STEP, LANES), 1)
 
     def group(g, carry):
-        start = pl.multiple_of(g * STEP, 8)
+        start = 0
         rows = pl.ds(start, STEP)
         cell = place[rows, :]
         code = codes_ref[0, 0, rows, :]
@@ -118,22 +120,33 @@
         d = dz >> 1
         low, first, third = d < 2, d < 1, d < 3
         left = lane_step < ROWS
-        tabs = []
+        both, third_of, colour_of = [], [], []
         for k in range(4):
-            at = pl.ds(pl.multiple_of(k * SLOTS + start, 8), STEP)
-            for pair in range(2):
-                cols = slice(pair * LANES, (pair + 1) * LANES)
-                even = window[0, at, cols]
-                odd = window[1, at, cols] if k < 3 else even
-                tabs.append((jnp.where(left, even, odd), jnp.where(left, odd, even)))
-        diff = []
-        for c in range(4):
-            mine = [tabs[2 * k + c // 2][c % 2] for k in range(4)]
-            got = [lane_take(t, index[c % 2]) for t in mine]
+            at = pl.ds(k * SLOTS, STEP)
+            even = [window[0, at, p * LANES : (p + 1) * LANES] for p in range(2)]
+            odd = [window[1, at, p * LANES : (p + 1) * LANES] for p in range(2)] if k < 3 else even
+            x_whole = jnp.where(left, even[0], odd[0]).astype(jnp.int32)
+            y_whole = jnp.where(left, even[1], odd[1]).astype(jnp.int32)
+            both.append((x_whole << 16) | y_whole)
+            third_of.append(jnp.where(left, odd[0], even[0]))
+            colour_of.append(jnp.where(left, odd[1], even[1]))
+
+        def pick(tabs, swapped):
+            got = [lane_take(t, index[swapped]) for t in tabs]
             value = jnp.where(
                 low, jnp.where(first, got[0], got[1]), jnp.where(third, got[2], got[3])
             )
-            diff.append(value - lane_take(mine[1], centre[c % 2]))
+            return value, lane_take(tabs[1], centre[swapped])
+
+        at_near, at_own = pick(both, 0)
+        z_near, z_own = pick(third_of, 1)
+        c_near, c_own = pick(colour_of, 1)
+        diff = (
+            ((at_near >> 16) - (at_own >> 16)).astype(jnp.float32) * (1.0 / SCALE),
+            ((at_near & 65535) - (at_own & 65535)).astype(jnp.float32) * (1.0 / SCALE),
+            z_near - z_own,
+            c_near - c_own,
+        )
         ox = (near_x - x).astype(jnp.float32) + diff[0]
         oy = (near_y - y).astype(jnp.float32) + diff[1]
         oz = (near_z - z).astype(jnp.float32) + diff[2]
@@ -147,14 +160,11 @@
         return carry
 
     moments[SLOTS:, :] = jnp.zeros((2 * LANES - SLOTS, LANES), jnp.float32)
-    copies[3].wait()
-    lax.fori_loop(0, SLOTS // STEP, group, 0)
+    group(0, 0)
 
     sums = jnp.concatenate([moments[0:LANES, :].T, moments[LANES:, :].T], axis=1)
     kappa = final_curvature(*[sums[q : q + 1, :] for q in range(10)])
     slot = lax.broadcasted_iota(jnp.int32, (1, 2 * LANES), 1)
-    for copy in copies[4:]:
-        copy.wait()
     kappa = jnp.where(slot < counts_ref[0, 0], kappa, 0.0)
     kappa_ref[0] = kappa[:, :SLOTS]
 

time: 22.7 us -> 21.9 us (0.965)
  Pallas kernels: 4.63 us -> 3.87 us
    pallas_call x1, Pallas kernels: 3.73 us -> 2.96 us  [curvature_call(): pl.pallas_call(curvature_kernel, out_shape=(jax.ShapeDtypeStruct((1, 1, S...]
where the time goes in v4:
time: 21.9 us; the launch traced here: 21.8 us
  starting transfers between devices  7.31 us (33%)
  blocking collectives  6.6 us (30%)
  Pallas kernels  3.87 us (18%)
  waiting for transfers between devices  2.67 us (12%)
  between operations  1.31 us (6%)
    ppermute x2, starting transfers between devices, swap_odd(): return lax.ppermute(value, axis, pairs)  7.31 us
    all_gather x2, blocking collectives, gather_even(): return lax.all_gather(value, axis, axis=0, axis_index_groups=groups)  6.6 us
    pallas_call x1, Pallas kernels, curvature_call(): pl.pallas_call(curvature_kernel, out_shape=(jax.ShapeDtypeStruct((1, 1, S...  2.96 us
    ppermute x2, waiting for transfers between devices, swap_odd(): return lax.ppermute(value, axis, pairs)  2.67 us
    pallas_call x1, Pallas kernels, sweeps_call(): pl.pallas_call(functools.partial(sweeps_kernel, n_gx, n_gy), out_shape=(j...  0.89 us
  transfers between devices with their start and end apart: 2, of which 1 were waited for; matrix products, arithmetic and copies ran while one was open for 0% of the time, Pallas kernels for 0%

profile of v4, /device:TPU:258, one launch (start us, length us, event | category | flops | bytes accessed | tf_op | source)
XLA Modules:
  0.0 21.8 jit_solution(9572938708064252412)
XLA Ops:
  1.3 3.0 %curvature.1 = (f32[1,1,192]{2,1,0:T(1,128)S(1)}, f32[8,8,128]{2,1,0:T(8,128)S(1)}, f32[8,8,128]{2,1,0:T(8,128)S(1)}, f32[5,8,128]{2,1,0:T(8,128)S(1)}, f32[5,8,128]{2,1,0:T(8,128)S(1)}) custom-call(f32[3,8,8,128]{3,2,1,0:T(8,128)} %jitter_hbm.1, f32[8,8,128]{2,1,0:T(8,128)} %colour_hbm.1, s32[1,1,192]{2,1,0:T(1,128)} %cells_hbm.1, ...), custom_call_target="tpu_custom_call" | custom-call | tf_op jit(solution)/shard_map/curvature/pallas_call | solution.py:200
  4.2 3.9 %collective-permute-start = (f32[5,8,128]{2,1,0:T(8,128)S(1)}, f32[5,8,128]{2,1,0:T(8,128)S(1)}, u32[]{:S(2)}, u32[]{:S(2)}) collective-permute-start(f32[5,8,128]{2,1,0:T(8,128)S(1)} %get-tuple-element.13), channel_id=1, source_target_pairs={{4,8},{8,4},{12,16},{16,12},{20,24},{24,20},{28,32},{32,28},{36,40... | collective-permute-start | bytes 61448 | tf_op jit(solution)/shard_map/ppermute | solution.py:307
  8.2 1.8 %all-gather = f32[10,8,128]{2,1,0:T(8,128)S(1)} all-gather(f32[5,8,128]{2,1,0:T(8,128)S(1)} %get-tuple-element.12), channel_id=2, replica_groups={{0,4},{8,12},{16,20},{24,28},{32,36},{40,44},{48,52},{56,60},{64,68},{7..., dimensions={0}, use_global_device_ids=true | all-gather | bytes 61440 | tf_op jit(solution)/shard_map/all_gather | solution.py:312
  10.0 2.7 %collective-permute-done.xo_ref = f32[5,8,128]{2,1,0:T(8,128)S(1)} collective-permute-done((f32[5,8,128]{2,1,0:T(8,128)S(1)}, f32[5,8,128]{2,1,0:T(8,128)S(1)}, u32[]{:S(2)}, u32[]{:S(2)}) %collective-permute-start) | collective-permute-done | bytes 20512 | tf_op jit(solution)/shard_map/ppermute | solution.py:307
  12.7 3.4 %collective-permute-start.1 = (f32[12,8,128]{2,1,0:T(8,128)S(1)}, f32[12,8,128]{2,1,0:T(8,128)S(1)}, u32[]{:S(2)}, u32[]{:S(2)}) collective-permute-start(f32[12,8,128]{2,1,0:T(8,128)S(1)} %get-tuple-element.15), channel_id=1, source_target_pairs={{1,2},{2,1},{5,6},{6,5},{9,10},{10,9},{13,14},{14,13},{17,18},{18,... | collective-permute-start | bytes 147464 | tf_op jit(solution)/shard_map/ppermute | solution.py:307
  16.1 4.8 %all-gather.1 = f32[24,8,128]{2,1,0:T(8,128)S(1)} all-gather(f32[12,8,128]{2,1,0:T(8,128)S(1)} %get-tuple-element.14), channel_id=3, replica_groups={{0,1},{2,3},{4,5},{6,7},{8,9},{10,11},{12,13},{14,15},{16,17},{18,19},{..., dimensions={0}, use_global_device_ids=true | all-gather | bytes 147456 | tf_op jit(solution)/shard_map/all_gather | solution.py:312
  20.9 0.0 collective-permute-done.1.yo_ref
  20.9 0.9 %sweeps.1 = (f32[8,8,128]{2,1,0:T(8,128)}, f32[1,1,192]{2,1,0:T(1,128)}) custom-call(f32[1,1,192]{2,1,0:T(1,128)S(1)} %get-tuple-element.9.kappa_ref, f32[8,8,128]{2,1,0:T(8,128)S(1)} %get-tuple-element.10.pressure_ref, f32[8,8,128]{2,1,0:T(8,128)S(1)} %get-tuple-element.11.rhs_ref, f32[2,5,8,128]{3,2,1,0:T(8,128)S(1)} %bitcast.4, ...), custom_call_target="tpu_custom_call" | custom-call | tf_op jit(solution)/shard_map/sweeps/pallas_call | solution.py:290
  (1 shorter events, 0.0 us)
Async XLA Ops:
  4.2 8.4 %collective-permute-start = (f32[5,8,128]{2,1,0:T(8,128)S(1)}, f32[5,8,128]{2,1,0:T(8,128)S(1)}, u32[]{:S(2)}, u32[]{:S(2)}) collective-permute-start(f32[5,8,128]{2,1,0:T(8,128)S(1)} %get-tuple-element.13), channel_id=1, source_target_pairs={{4,8},{8,4},{12,16},{16,12},{20,24},{24,20},{28,32},{32,28},{36,40... | collective-permute-start | bytes 61448 | tf_op jit(solution)/shard_map/ppermute | solution.py:307
  12.7 8.2 %collective-permute-start.1 = (f32[12,8,128]{2,1,0:T(8,128)S(1)}, f32[12,8,128]{2,1,0:T(8,128)S(1)}, u32[]{:S(2)}, u32[]{:S(2)}) collective-permute-start(f32[12,8,128]{2,1,0:T(8,128)S(1)} %get-tuple-element.15), channel_id=1, source_target_pairs={{1,2},{2,1},{5,6},{6,5},{9,10},{10,9},{13,14},{14,13},{17,18},{18,... | collective-permute-start | bytes 147464 | tf_op jit(solution)/shard_map/ppermute | solution.py:307

commit v5 on v4

--- a/solution.py
+++ b/solution.py
@@ -225,24 +225,36 @@
     return jnp.where(even, second, first), jnp.where(even, first, second)
 
 
-def middle_kernel(pressure_ref, rhs_ref, xe_ref, xo_ref, even_ref, odd_ref):
+CORNERS = (
+    (False, 1, 0), (False, 2, 0), (False, 2, 1), (False, 4, 0),
+    (True, 0, 0), (True, 0, 1), (True, 3, 0), (True, 1, 0),
+)
+
+
+def edges_kernel(pressure_ref, rhs_ref, xe_ref, xo_ref, even_ref, odd_ref):
     odd_x = lax.rem(lax.axis_index("gx"), 2)
     even_y = lax.rem(lax.axis_index("gy"), 2) == 0
-    below, above = sides(xe_ref[1 - odd_x], xo_ref[...], odd_x == 0)
-    planes = jnp.concatenate([below[1:3], pressure_ref[...], above[0:2]], axis=0)
-    rhs = jnp.concatenate([below[3:5], rhs_ref[...], above[3:5]], axis=0)
-    sub = lax.broadcasted_iota(jnp.int32, (1, 8, LANES), 1)
-    high = jnp.where(sub >= 5, planes, pltpu.roll(rhs, 5, 1))
-    low = jnp.where(sub < 3, planes, pltpu.roll(rhs, 3, 1))
-    even_ref[...] = jnp.where(even_y, high, low)
-    odd_ref[...] = jnp.where(even_y, low, high)
-
-
-def middle_call(pressure, rhs, xe, xo):
+
+    def send(tile, rows, high, low):
+        even_ref[tile, rows] = jnp.where(even_y, high, low)
+        odd_ref[tile, rows] = jnp.where(even_y, low, high)
+
+    for tile in range(5):
+        ref, away = (pressure_ref, tile) if tile < 3 else (rhs_ref, tile - 3)
+        send(tile, slice(0, 8), ref[:, 7 - away, :], ref[:, away, :])
+    for at, (above, tile, away) in enumerate(CORNERS):
+        ends = []
+        for row in (7 - away, away):
+            pair = (xe_ref[1 - odd_x, tile, row : row + 1, :], xo_ref[tile, row : row + 1, :])
+            ends.append(sides(*pair, odd_x == 0)[int(above)])
+        send(5, slice(at, at + 1), *ends)
+
+
+def edges_call(pressure, rhs, xe, xo):
     vmem = pl.BlockSpec(memory_space=pltpu.VMEM)
-    strip = jax.ShapeDtypeStruct((12, 8, LANES), jnp.float32)
+    strip = jax.ShapeDtypeStruct((6, 8, LANES), jnp.float32)
     return pl.pallas_call(
-        middle_kernel,
+        edges_kernel,
         out_shape=(strip, strip),
         in_specs=[vmem] * 4,
         out_specs=(vmem, vmem),
@@ -253,27 +265,38 @@
 
 def sweeps_kernel(
     n_gx, n_gy, kappa_ref, pressure_ref, rhs_ref, xe_ref, xo_ref, ye_ref, yo_ref,
-    out_ref, curvature_ref,
+    out_ref, curvature_ref, wide, source,
 ):
     at_x, at_y = lax.axis_index("gx"), lax.axis_index("gy")
     odd_x, odd_y = lax.rem(at_x, 2), lax.rem(at_y, 2)
     below, above = sides(xe_ref[1 - odd_x], xo_ref[...], odd_x == 0)
     left, right = sides(ye_ref[1 - odd_y], yo_ref[...], odd_y == 0)
     curvature_ref[...] = kappa_ref[...]
-    own = jnp.concatenate([below[0:3], pressure_ref[...], above[0:3]], axis=0)
-    rhs = jnp.concatenate([below[3:5], rhs_ref[...], above[3:5]], axis=0)
-    nothing = jnp.zeros((1, 8, LANES), jnp.float32)
-    wide_left = jnp.concatenate([nothing, left, nothing], axis=0)
-    wide_right = jnp.concatenate([nothing, right, nothing], axis=0)
-    current = jnp.concatenate([wide_left, own, wide_right], axis=1)
-    rhs = jnp.concatenate([pltpu.roll(left, 3, 1), rhs, pltpu.roll(right, 5, 1)], axis=1)
-    lane = lax.broadcasted_iota(jnp.int32, (1, 24, LANES), 2)
-    sub = lax.broadcasted_iota(jnp.int32, (1, 24, LANES), 1)
-    inside = (jnp.where(at_y > 0, 0, 8) <= sub) & (sub < jnp.where(at_y < n_gy - 1, 24, 16))
+    wide[:, 8:, :] = jnp.zeros((14, 8, LANES), jnp.float32)
+    source[:, 8:, :] = jnp.zeros((12, 8, LANES), jnp.float32)
+    wide[0:3, 0:8, :], wide[3:11, 0:8, :], wide[11:14, 0:8, :] = below[0:3], pressure_ref[...], above[0:3]
+    source[0:2, 0:8, :], source[2:10, 0:8, :], source[10:12, 0:8, :] = below[3:5], rhs_ref[...], above[3:5]
+    for part, rows in ((right, (8, 9, 10)), (left, (15, 14, 13))):
+        for tile in range(3):
+            wide[3:11, rows[tile], :] = part[tile]
+        for tile in range(2):
+            source[2:10, rows[tile], :] = part[3 + tile]
+        for at, (high, tile, away) in enumerate(CORNERS):
+            row = rows[away]
+            if tile < 3:
+                plane = 11 + tile if high else tile
+                wide[plane, row : row + 1, :] = part[5, at : at + 1]
+            else:
+                plane = 10 + tile - 3 if high else tile - 3
+                source[plane, row : row + 1, :] = part[5, at : at + 1]
+    current, rhs = wide[...], source[...]
+    lane = lax.broadcasted_iota(jnp.int32, (1, 16, LANES), 2)
+    sub = lax.broadcasted_iota(jnp.int32, (1, 16, LANES), 1)
+    inside = (sub < jnp.where(at_y < n_gy - 1, 12, 8)) | (sub >= jnp.where(at_y > 0, 12, 16))
     for sweep in range(3):
         mid = current[1:-1]
         beside = current[2:] + current[:-2]
-        beside = beside + pltpu.roll(mid, 23, 1) + pltpu.roll(mid, 1, 1)
+        beside = beside + pltpu.roll(mid, 15, 1) + pltpu.roll(mid, 1, 1)
         beside = beside + jnp.where(lane < LANES - 1, pltpu.roll(mid, LANES - 1, 2), 0.0)
         beside = beside + jnp.where(lane > 0, pltpu.roll(mid, 1, 2), 0.0)
         current = (beside + rhs[sweep : 12 - sweep]) / 6.0
@@ -282,7 +305,7 @@
             plane = lax.broadcasted_iota(jnp.int32, (count, 1, 1), 0) + (sweep - 2)
             held = (plane >= jnp.where(at_x > 0, -2, 0)) & (plane < jnp.where(at_x < n_gx - 1, 10, 8))
             current = jnp.where(held & inside, current, 0.0)
-    out_ref[...] = current[:, 8:16, :]
+    out_ref[...] = current[:, 0:8, :]
 
 
 def sweeps_call(n_gx, n_gy, *values):
@@ -295,6 +318,10 @@
         ),
         in_specs=[vmem] * 7,
         out_specs=(vmem, vmem),
+        scratch_shapes=[
+            pltpu.VMEM((14, 16, LANES), jnp.float32),
+            pltpu.VMEM((12, 16, LANES), jnp.float32),
+        ],
         compiler_params=pltpu.CompilerParams(vmem_limit_bytes=8 * 2**20),
         name="sweeps",
     )(*values)
@@ -322,7 +349,7 @@
         counts, held(source), held(pressure),
     )
     xo, xe = swap_odd(odd, "gx"), gather_even(even, "gx")
-    even, odd = middle_call(own, rhs, xe, xo)
+    even, odd = edges_call(own, rhs, xe, xo)
     yo, ye = swap_odd(odd, "gy"), gather_even(even, "gy")
     return sweeps_call(
         lax.axis_size("gx"), lax.axis_size("gy"), kappa, own, rhs, xe, xo, ye, yo

time: 21.9 us -> 21.7 us (level)
  blocking collectives: 6.6 us -> 6.34 us
    all_gather x2, blocking collectives: 6.6 us -> 6.34 us  [gather_even(): return lax.all_gather(value, axis, axis=0, axis_index_groups=groups)]
where the time goes in v5:
time: 21.7 us; the launch traced here: 21.5 us
  starting transfers between devices  7.31 us (34%)
  blocking collectives  6.34 us (29%)
  Pallas kernels  3.88 us (18%)
  waiting for transfers between devices  2.67 us (12%)
  between operations  1.31 us (6%)
    ppermute x2, starting transfers between devices, swap_odd(): return lax.ppermute(value, axis, pairs)  7.31 us
    all_gather x2, blocking collectives, gather_even(): return lax.all_gather(value, axis, axis=0, axis_index_groups=groups)  6.34 us
    pallas_call x1, Pallas kernels, curvature_call(): pl.pallas_call(curvature_kernel, out_shape=(jax.ShapeDtypeStruct((1, 1, S...  2.96 us
    ppermute x2, waiting for transfers between devices, swap_odd(): return lax.ppermute(value, axis, pairs)  2.67 us
    pallas_call x1, Pallas kernels, sweeps_call(): pl.pallas_call(functools.partial(sweeps_kernel, n_gx, n_gy), out_shape=(j...  0.87 us
  transfers between devices with their start and end apart: 2, of which 1 were waited for; matrix products, arithmetic and copies ran while one was open for 0% of the time, Pallas kernels for 0%

profile of v5, /device:TPU:258, one launch (start us, length us, event | category | flops | bytes accessed | tf_op | source)
XLA Modules:
  0.0 21.5 jit_solution(4356232085944726313)
XLA Ops:
  1.3 3.0 %curvature.1 = (f32[1,1,192]{2,1,0:T(1,128)S(1)}, f32[8,8,128]{2,1,0:T(8,128)S(1)}, f32[8,8,128]{2,1,0:T(8,128)S(1)}, f32[5,8,128]{2,1,0:T(8,128)S(1)}, f32[5,8,128]{2,1,0:T(8,128)S(1)}) custom-call(f32[3,8,8,128]{3,2,1,0:T(8,128)} %jitter_hbm.1, f32[8,8,128]{2,1,0:T(8,128)} %colour_hbm.1, s32[1,1,192]{2,1,0:T(1,128)} %cells_hbm.1, ...), custom_call_target="tpu_custom_call" | custom-call | tf_op jit(solution)/shard_map/curvature/pallas_call | solution.py:200
  4.2 3.9 %collective-permute-start = (f32[5,8,128]{2,1,0:T(8,128)S(1)}, f32[5,8,128]{2,1,0:T(8,128)S(1)}, u32[]{:S(2)}, u32[]{:S(2)}) collective-permute-start(f32[5,8,128]{2,1,0:T(8,128)S(1)} %get-tuple-element.13), channel_id=1, source_target_pairs={{4,8},{8,4},{12,16},{16,12},{20,24},{24,20},{28,32},{32,28},{36,40... | collective-permute-start | bytes 61448 | tf_op jit(solution)/shard_map/ppermute | solution.py:334
  8.2 1.8 %all-gather = f32[10,8,128]{2,1,0:T(8,128)S(1)} all-gather(f32[5,8,128]{2,1,0:T(8,128)S(1)} %get-tuple-element.12), channel_id=2, replica_groups={{0,4},{8,12},{16,20},{24,28},{32,36},{40,44},{48,52},{56,60},{64,68},{7..., dimensions={0}, use_global_device_ids=true | all-gather | bytes 61440 | tf_op jit(solution)/shard_map/all_gather | solution.py:339
  10.0 2.7 %collective-permute-done.xo_ref = f32[5,8,128]{2,1,0:T(8,128)S(1)} collective-permute-done((f32[5,8,128]{2,1,0:T(8,128)S(1)}, f32[5,8,128]{2,1,0:T(8,128)S(1)}, u32[]{:S(2)}, u32[]{:S(2)}) %collective-permute-start) | collective-permute-done | bytes 20512 | tf_op jit(solution)/shard_map/ppermute | solution.py:334
  12.7 3.4 %collective-permute-start.1 = (f32[6,8,128]{2,1,0:T(8,128)S(1)}, f32[6,8,128]{2,1,0:T(8,128)S(1)}, u32[]{:S(2)}, u32[]{:S(2)}) collective-permute-start(f32[6,8,128]{2,1,0:T(8,128)S(1)} %get-tuple-element.15), channel_id=1, source_target_pairs={{1,2},{2,1},{5,6},{6,5},{9,10},{10,9},{13,14},{14,13},{17,18},{18,... | collective-permute-start | bytes 73736 | tf_op jit(solution)/shard_map/ppermute | solution.py:334
  16.1 4.5 %all-gather.1 = f32[12,8,128]{2,1,0:T(8,128)S(1)} all-gather(f32[6,8,128]{2,1,0:T(8,128)S(1)} %get-tuple-element.14), channel_id=3, replica_groups={{0,1},{2,3},{4,5},{6,7},{8,9},{10,11},{12,13},{14,15},{16,17},{18,19},{..., dimensions={0}, use_global_device_ids=true | all-gather | bytes 73728 | tf_op jit(solution)/shard_map/all_gather | solution.py:339
  20.6 0.0 collective-permute-done.1.yo_ref
  20.6 0.9 %sweeps.1 = (f32[8,8,128]{2,1,0:T(8,128)}, f32[1,1,192]{2,1,0:T(1,128)}) custom-call(f32[1,1,192]{2,1,0:T(1,128)S(1)} %get-tuple-element.9.kappa_ref, f32[8,8,128]{2,1,0:T(8,128)S(1)} %get-tuple-element.10.pressure_ref, f32[8,8,128]{2,1,0:T(8,128)S(1)} %get-tuple-element.11.rhs_ref, f32[2,5,8,128]{3,2,1,0:T(8,128)S(1)} %bitcast.3, ...), custom_call_target="tpu_custom_call" | custom-call | tf_op jit(solution)/shard_map/sweeps/pallas_call | solution.py:313
  (1 shorter events, 0.0 us)
Async XLA Ops:
  4.2 8.4 %collective-permute-start = (f32[5,8,128]{2,1,0:T(8,128)S(1)}, f32[5,8,128]{2,1,0:T(8,128)S(1)}, u32[]{:S(2)}, u32[]{:S(2)}) collective-permute-start(f32[5,8,128]{2,1,0:T(8,128)S(1)} %get-tuple-element.13), channel_id=1, source_target_pairs={{4,8},{8,4},{12,16},{16,12},{20,24},{24,20},{28,32},{32,28},{36,40... | collective-permute-start | bytes 61448 | tf_op jit(solution)/shard_map/ppermute | solution.py:334
  12.7 7.9 %collective-permute-start.1 = (f32[6,8,128]{2,1,0:T(8,128)S(1)}, f32[6,8,128]{2,1,0:T(8,128)S(1)}, u32[]{:S(2)}, u32[]{:S(2)}) collective-permute-start(f32[6,8,128]{2,1,0:T(8,128)S(1)} %get-tuple-element.15), channel_id=1, source_target_pairs={{1,2},{2,1},{5,6},{6,5},{9,10},{10,9},{13,14},{14,13},{17,18},{18,... | collective-permute-start | bytes 73736 | tf_op jit(solution)/shard_map/ppermute | solution.py:334

commit v6 on v5

--- a/solution.py
+++ b/solution.py
@@ -12,7 +12,7 @@
 SLOTS = 192
 LANES = 128
 ROWS = 64
-STEP = 192
+FEW = 64
 SCALE = 32767.0 / 0.3
 
 
@@ -43,66 +43,22 @@
     return -(trace - quad / denom) / jnp.sqrt(denom)
 
 
-def curvature_kernel(
-    jitter_hbm, colour_hbm, cells_hbm, codes_hbm, counts_ref, source_hbm, pressure_hbm,
-    kappa_ref, own_ref, rhs_ref, even_ref, odd_ref,
-    jitter_ref, colour_ref, cells_ref, codes_ref, source_ref, arrived,
-    table, hot, window, place, row, moments,
-):
-    copies = [
-        pltpu.make_async_copy(source, target, arrived.at[i])
-        for i, (source, target) in enumerate((
-            (cells_hbm, cells_ref),
-            (jitter_hbm, jitter_ref),
-            (colour_hbm, colour_ref),
-            (codes_hbm, codes_ref),
-            (source_hbm, source_ref),
-            (pressure_hbm, own_ref),
-        ))
-    ]
-    for copy in copies:
-        copy.start()
-
-    copies[0].wait()
-    row[...] = jnp.zeros_like(row)
-    row[0:1, 0:SLOTS] = cells_ref[0]
-    cells_row = row[0:1, :]
-    as_float = cells_row.astype(jnp.float32)
-    for h in range(2):
-        part = jnp.broadcast_to(as_float[:, h * LANES : (h + 1) * LANES], (LANES, LANES))
-        turned = part.T.astype(jnp.int32)
-        keep = min(LANES, SLOTS - h * LANES)
-        place[h * LANES : h * LANES + keep, :] = turned[:keep]
-
-    lane = lax.broadcasted_iota(jnp.int32, (SLOTS, LANES), 1)
-    z_of = place[...] & 127
-    for step in range(7):
-        target = jnp.clip(z_of + (step - 3), 0, LANES - 1)
-        one = jnp.where(lane == target, 1.0, 0.0).astype(jnp.bfloat16)
-        for q in range(3):
-            hot[step % 2, (step // 2) * SLOTS : (step // 2 + 1) * SLOTS, q * LANES : (q + 1) * LANES] = one
-
-    for copy in copies[1:]:
-        copy.wait()
-    whole_x = jnp.round(jitter_ref[0] * SCALE)
-    whole_y = jnp.round(jitter_ref[1] * SCALE) + 32768.0
-    for c, value in enumerate((whole_x, jitter_ref[2], whole_y, colour_ref[...])):
-        for q, piece in enumerate(pieces(value.reshape(ROWS, LANES))):
-            columns = slice(q * LANES, (q + 1) * LANES)
-            table[0, c * ROWS : (c + 1) * ROWS, columns] = piece
-            table[1, (c ^ 1) * ROWS : ((c ^ 1) + 1) * ROWS, columns] = piece
-
+def curvature_of(size, count, codes_ref, kappa_ref, table, hot, window, place, row, moments, added):
     contract = (((1,), (1,)), ((), ()))
-    window[0] = lax.dot_general(hot[0], table[0], contract, preferred_element_type=jnp.float32)
-    window[1, : 3 * SLOTS] = lax.dot_general(
-        hot[1, : 3 * SLOTS], table[1], contract, preferred_element_type=jnp.float32
-    )
-
-    lane_step = lax.broadcasted_iota(jnp.int32, (STEP, LANES), 1)
-
-    def group(g, carry):
-        start = 0
-        rows = pl.ds(start, STEP)
+    width = -(-size // LANES) * LANES
+
+    for parity, steps in ((0, 4), (1, 3)):
+        starts = [k * SLOTS for k in range(steps)]
+        some = [hot[parity, at : at + size] for at in starts]
+        window[parity, : steps * size] = lax.dot_general(
+            jnp.concatenate(some, axis=0), table[parity], contract,
+            preferred_element_type=jnp.float32,
+        )
+
+    lane_step = lax.broadcasted_iota(jnp.int32, (size, LANES), 1)
+
+    def group():
+        rows = slice(0, size)
         cell = place[rows, :]
         code = codes_ref[0, 0, rows, :]
         x, y, z = cell >> 10, (cell >> 7) & 7, cell & 127
@@ -122,7 +78,7 @@
         left = lane_step < ROWS
         both, third_of, colour_of = [], [], []
         for k in range(4):
-            at = pl.ds(k * SLOTS, STEP)
+            at = slice(k * size, (k + 1) * size)
             even = [window[0, at, p * LANES : (p + 1) * LANES] for p in range(2)]
             odd = [window[1, at, p * LANES : (p + 1) * LANES] for p in range(2)] if k < 3 else even
             x_whole = jnp.where(left, even[0], odd[0]).astype(jnp.int32)
@@ -153,32 +109,91 @@
         w = diff[3] * jnp.exp(-(ox * ox + oy * oy + oz * oz) / SMOOTH_SQ)
         wx, wy, wz = w * ox, w * oy, w * oz
         terms = (w, wx, wy, wz, wx * ox, wy * oy, wz * oz, wx * oy, wx * oz, wy * oz)
-        out = jnp.zeros((STEP, LANES), jnp.float32)
+        out = jnp.zeros((size, LANES), jnp.float32)
         for q, term in enumerate(terms):
             out = jnp.where(lane_step == q, jnp.sum(term, axis=1, keepdims=True), out)
         moments[rows, :] = out
-        return carry
-
-    moments[SLOTS:, :] = jnp.zeros((2 * LANES - SLOTS, LANES), jnp.float32)
-    group(0, 0)
-
-    sums = jnp.concatenate([moments[0:LANES, :].T, moments[LANES:, :].T], axis=1)
+
+    moments[size:width, :] = jnp.zeros((width - size, LANES), jnp.float32)
+    group()
+
+    blocks = [slice(at, at + LANES) for at in range(0, width, LANES)]
+    sums = jnp.concatenate([moments[block, :].T for block in blocks], axis=1)
     kappa = final_curvature(*[sums[q : q + 1, :] for q in range(10)])
-    slot = lax.broadcasted_iota(jnp.int32, (1, 2 * LANES), 1)
-    kappa = jnp.where(slot < counts_ref[0, 0], kappa, 0.0)
-    kappa_ref[0] = kappa[:, :SLOTS]
-
-    sub = lax.broadcasted_iota(jnp.int32, (ROWS, 2 * LANES), 0)
-    spread = jnp.where(sub == (cells_row >> 7), SIGMA * kappa, 0.0)
-    added = jnp.zeros((ROWS, LANES), jnp.float32)
+    slot = lax.broadcasted_iota(jnp.int32, (1, width), 1)
+    kappa = jnp.where(slot < count, kappa, 0.0)
+    whole = jnp.concatenate([kappa, jnp.zeros((1, 2 * LANES), jnp.float32)], axis=1)
+    kappa_ref[0] = whole[:, :SLOTS]
+
+    sub = lax.broadcasted_iota(jnp.int32, (ROWS, width), 0)
+    spread = jnp.where(sub == (row[0:1, :width] >> 7), SIGMA * kappa, 0.0)
+    total = jnp.zeros((ROWS, LANES), jnp.float32)
     for piece in pieces(spread):
-        added = added + jnp.dot(
-            piece[:, :LANES], hot[1, SLOTS : SLOTS + LANES, :LANES], preferred_element_type=jnp.float32
-        )
-        added = added + jnp.dot(
-            piece[:, LANES:SLOTS], hot[1, SLOTS + LANES : 2 * SLOTS, :LANES], preferred_element_type=jnp.float32
-        )
-    rhs = source_ref[...] + added.reshape(8, 8, LANES)
+        for block in blocks:
+            end = min(block.stop, SLOTS)
+            total = total + jnp.dot(
+                piece[:, block.start : end],
+                hot[1, SLOTS + block.start : SLOTS + end, :LANES],
+                preferred_element_type=jnp.float32,
+            )
+    added[...] = total
+
+
+def curvature_kernel(
+    jitter_hbm, colour_hbm, cells_hbm, codes_hbm, counts_ref, source_hbm, pressure_hbm,
+    kappa_ref, own_ref, rhs_ref, even_ref, odd_ref,
+    jitter_ref, colour_ref, cells_ref, codes_ref, source_ref, arrived,
+    table, hot, window, place, row, moments, added,
+):
+    copies = [
+        pltpu.make_async_copy(source, target, arrived.at[i])
+        for i, (source, target) in enumerate((
+            (cells_hbm, cells_ref),
+            (jitter_hbm, jitter_ref),
+            (colour_hbm, colour_ref),
+            (codes_hbm, codes_ref),
+            (source_hbm, source_ref),
+            (pressure_hbm, own_ref),
+        ))
+    ]
+    for copy in copies:
+        copy.start()
+
+    copies[0].wait()
+    row[...] = jnp.zeros_like(row)
+    row[0:1, 0:SLOTS] = cells_ref[0]
+    cells_row = row[0:1, :]
+    as_float = cells_row.astype(jnp.float32)
+    for h in range(2):
+        part = jnp.broadcast_to(as_float[:, h * LANES : (h + 1) * LANES], (LANES, LANES))
+        turned = part.T.astype(jnp.int32)
+        keep = min(LANES, SLOTS - h * LANES)
+        place[h * LANES : h * LANES + keep, :] = turned[:keep]
+
+    lane = lax.broadcasted_iota(jnp.int32, (SLOTS, LANES), 1)
+    z_of = place[...] & 127
+    for step in range(7):
+        target = jnp.clip(z_of + (step - 3), 0, LANES - 1)
+        one = jnp.where(lane == target, 1.0, 0.0).astype(jnp.bfloat16)
+        for q in range(3):
+            hot[step % 2, (step // 2) * SLOTS : (step // 2 + 1) * SLOTS, q * LANES : (q + 1) * LANES] = one
+
+    for copy in copies[1:]:
+        copy.wait()
+    whole_x = jnp.round(jitter_ref[0] * SCALE)
+    whole_y = jnp.round(jitter_ref[1] * SCALE) + 32768.0
+    for c, value in enumerate((whole_x, jitter_ref[2], whole_y, colour_ref[...])):
+        for q, piece in enumerate(pieces(value.reshape(ROWS, LANES))):
+            columns = slice(q * LANES, (q + 1) * LANES)
+            table[0, c * ROWS : (c + 1) * ROWS, columns] = piece
+            table[1, (c ^ 1) * ROWS : ((c ^ 1) + 1) * ROWS, columns] = piece
+
+    count = counts_ref[0, 0]
+    rest = (codes_ref, kappa_ref, table, hot, window, place, row, moments, added)
+    pl.when(count <= FEW)(lambda: curvature_of(FEW, count, *rest))
+    pl.when(count > FEW)(lambda: curvature_of(SLOTS, count, *rest))
+
+    rhs = source_ref[...] + added[...].reshape(8, 8, LANES)
     rhs_ref[...] = rhs
     even = lax.rem(lax.axis_index("gx"), 2) == 0
     pressure = own_ref[...]
@@ -215,6 +230,7 @@
             pltpu.VMEM((SLOTS, LANES), jnp.int32),
             pltpu.VMEM((8, 2 * LANES), jnp.int32),
             pltpu.VMEM((2 * LANES, LANES), jnp.float32),
+            pltpu.VMEM((ROWS, LANES), jnp.float32),
         ],
         compiler_params=pltpu.CompilerParams(vmem_limit_bytes=16 * 2**20),
         name="curvature",

time: 21.7 us -> 20.9 us (0.963)
  starting transfers between devices: 7.31 us -> 5.57 us
  waiting for transfers between devices: 2.67 us -> 3.32 us
  blocking collectives: 6.34 us -> 6.56 us
    ppermute x2, starting transfers between devices: 7.31 us -> 5.57 us  [swap_odd(): return lax.ppermute(value, axis, pairs)]
    ppermute x2, waiting for transfers between devices: 2.67 us -> 3.32 us  [swap_odd(): return lax.ppermute(value, axis, pairs)]
    all_gather x2, blocking collectives: 6.34 us -> 6.56 us  [gather_even(): return lax.all_gather(value, axis, axis=0, axis_index_groups=groups)]
where the time goes in v6:
time: 20.9 us; the launch traced here: 20.7 us
  blocking collectives  6.56 us (31%)
  starting transfers between devices  5.57 us (27%)
  Pallas kernels  3.92 us (19%)
  waiting for transfers between devices  3.32 us (16%)
  between operations  1.31 us (6%)
    all_gather x2, blocking collectives, gather_even(): return lax.all_gather(value, axis, axis=0, axis_index_groups=groups)  6.56 us
    ppermute x2, starting transfers between devices, swap_odd(): return lax.ppermute(value, axis, pairs)  5.57 us
    ppermute x2, waiting for transfers between devices, swap_odd(): return lax.ppermute(value, axis, pairs)  3.32 us
    pallas_call x1, Pallas kernels, curvature_call(): pl.pallas_call(curvature_kernel, out_shape=(jax.ShapeDtypeStruct((1, 1, S...  3 us
    pallas_call x1, Pallas kernels, sweeps_call(): pl.pallas_call(functools.partial(sweeps_kernel, n_gx, n_gy), out_shape=(j...  0.87 us
  transfers between devices with their start and end apart: 2, of which 1 were waited for; matrix products, arithmetic and copies ran while one was open for 0% of the time, Pallas kernels for 0%

profile of v6, /device:TPU:258, one launch (start us, length us, event | category | flops | bytes accessed | tf_op | source)
XLA Modules:
  0.0 20.7 jit_solution(1249435869263419764)
XLA Ops:
  1.3 3.0 %curvature.1 = (f32[1,1,192]{2,1,0:T(1,128)S(1)}, f32[8,8,128]{2,1,0:T(8,128)S(1)}, f32[8,8,128]{2,1,0:T(8,128)S(1)}, f32[5,8,128]{2,1,0:T(8,128)S(1)}, f32[5,8,128]{2,1,0:T(8,128)S(1)}) custom-call(f32[3,8,8,128]{3,2,1,0:T(8,128)} %jitter_hbm.1, f32[8,8,128]{2,1,0:T(8,128)} %colour_hbm.1, s32[1,1,192]{2,1,0:T(1,128)} %cells_hbm.1, ...), custom_call_target="tpu_custom_call" | custom-call | tf_op jit(solution)/shard_map/curvature/pallas_call | solution.py:215
  4.3 3.0 %collective-permute-start = (f32[5,8,128]{2,1,0:T(8,128)S(1)}, f32[5,8,128]{2,1,0:T(8,128)S(1)}, u32[]{:S(2)}, u32[]{:S(2)}) collective-permute-start(f32[5,8,128]{2,1,0:T(8,128)S(1)} %get-tuple-element.13), channel_id=1, source_target_pairs={{4,8},{8,4},{12,16},{16,12},{20,24},{24,20},{28,32},{32,28},{36,40... | collective-permute-start | bytes 61448 | tf_op jit(solution)/shard_map/ppermute | solution.py:350
  7.3 2.1 %all-gather = f32[10,8,128]{2,1,0:T(8,128)S(1)} all-gather(f32[5,8,128]{2,1,0:T(8,128)S(1)} %get-tuple-element.12), channel_id=2, replica_groups={{0,4},{8,12},{16,20},{24,28},{32,36},{40,44},{48,52},{56,60},{64,68},{7..., dimensions={0}, use_global_device_ids=true | all-gather | bytes 61440 | tf_op jit(solution)/shard_map/all_gather | solution.py:355
  9.4 3.3 %collective-permute-done.xo_ref = f32[5,8,128]{2,1,0:T(8,128)S(1)} collective-permute-done((f32[5,8,128]{2,1,0:T(8,128)S(1)}, f32[5,8,128]{2,1,0:T(8,128)S(1)}, u32[]{:S(2)}, u32[]{:S(2)}) %collective-permute-start) | collective-permute-done | bytes 20512 | tf_op jit(solution)/shard_map/ppermute | solution.py:350
  12.8 2.5 %collective-permute-start.1 = (f32[6,8,128]{2,1,0:T(8,128)S(1)}, f32[6,8,128]{2,1,0:T(8,128)S(1)}, u32[]{:S(2)}, u32[]{:S(2)}) collective-permute-start(f32[6,8,128]{2,1,0:T(8,128)S(1)} %get-tuple-element.15), channel_id=1, source_target_pairs={{1,2},{2,1},{5,6},{6,5},{9,10},{10,9},{13,14},{14,13},{17,18},{18,... | collective-permute-start | bytes 73736 | tf_op jit(solution)/shard_map/ppermute | solution.py:350
  15.3 4.5 %all-gather.1 = f32[12,8,128]{2,1,0:T(8,128)S(1)} all-gather(f32[6,8,128]{2,1,0:T(8,128)S(1)} %get-tuple-element.14), channel_id=3, replica_groups={{0,1},{2,3},{4,5},{6,7},{8,9},{10,11},{12,13},{14,15},{16,17},{18,19},{..., dimensions={0}, use_global_device_ids=true | all-gather | bytes 73728 | tf_op jit(solution)/shard_map/all_gather | solution.py:355
  19.8 0.0 collective-permute-done.1.yo_ref
  19.8 0.9 %sweeps.1 = (f32[8,8,128]{2,1,0:T(8,128)}, f32[1,1,192]{2,1,0:T(1,128)}) custom-call(f32[1,1,192]{2,1,0:T(1,128)S(1)} %get-tuple-element.9.kappa_ref, f32[8,8,128]{2,1,0:T(8,128)S(1)} %get-tuple-element.10.pressure_ref, f32[8,8,128]{2,1,0:T(8,128)S(1)} %get-tuple-element.11.rhs_ref, f32[2,5,8,128]{3,2,1,0:T(8,128)S(1)} %bitcast.3, ...), custom_call_target="tpu_custom_call" | custom-call | tf_op jit(solution)/shard_map/sweeps/pallas_call | solution.py:329
  (1 shorter events, 0.0 us)
Async XLA Ops:
  4.3 8.4 %collective-permute-start = (f32[5,8,128]{2,1,0:T(8,128)S(1)}, f32[5,8,128]{2,1,0:T(8,128)S(1)}, u32[]{:S(2)}, u32[]{:S(2)}) collective-permute-start(f32[5,8,128]{2,1,0:T(8,128)S(1)} %get-tuple-element.13), channel_id=1, source_target_pairs={{4,8},{8,4},{12,16},{16,12},{20,24},{24,20},{28,32},{32,28},{36,40... | collective-permute-start | bytes 61448 | tf_op jit(solution)/shard_map/ppermute | solution.py:350
  12.8 7.0 %collective-permute-start.1 = (f32[6,8,128]{2,1,0:T(8,128)S(1)}, f32[6,8,128]{2,1,0:T(8,128)S(1)}, u32[]{:S(2)}, u32[]{:S(2)}) collective-permute-start(f32[6,8,128]{2,1,0:T(8,128)S(1)} %get-tuple-element.15), channel_id=1, source_target_pairs={{1,2},{2,1},{5,6},{6,5},{9,10},{10,9},{13,14},{14,13},{17,18},{18,... | collective-permute-start | bytes 73736 | tf_op jit(solution)/shard_map/ppermute | solution.py:350

commit v7 on v6

--- a/solution.py
+++ b/solution.py
@@ -12,7 +12,7 @@
 SLOTS = 192
 LANES = 128
 ROWS = 64
-FEW = 64
+SIZES = (32, 64)
 SCALE = 32767.0 / 0.3
 
 
@@ -109,34 +109,24 @@
         w = diff[3] * jnp.exp(-(ox * ox + oy * oy + oz * oz) / SMOOTH_SQ)
         wx, wy, wz = w * ox, w * oy, w * oz
         terms = (w, wx, wy, wz, wx * ox, wy * oy, wz * oz, wx * oy, wx * oz, wy * oz)
-        out = jnp.zeros((size, LANES), jnp.float32)
-        for q, term in enumerate(terms):
-            out = jnp.where(lane_step == q, jnp.sum(term, axis=1, keepdims=True), out)
-        moments[rows, :] = out
-
+        return [jnp.sum(term, axis=1, keepdims=True) for term in terms]
+
+    slot = lax.broadcasted_iota(jnp.int32, (size, 1), 0)
+    kappa = jnp.where(slot < count, final_curvature(*group()), 0.0)
+
+    sub = lax.broadcasted_iota(jnp.int32, (ROWS, width), 0)
+    row_hot = jnp.where(sub == (row[0:1, :width] >> 7), 1.0, 0.0).astype(jnp.bfloat16)[:, :size]
+    spread = jnp.where(lane_step == (place[0:size, :] & 127), SIGMA * kappa, 0.0)
+    parts = jnp.dot(
+        row_hot, jnp.concatenate(pieces(spread), axis=1), preferred_element_type=jnp.float32
+    )
+    added[...] = parts[:, :LANES] + parts[:, LANES : 2 * LANES] + parts[:, 2 * LANES :]
+
+    moments[0:size, :] = jnp.broadcast_to(kappa, (size, LANES))
     moments[size:width, :] = jnp.zeros((width - size, LANES), jnp.float32)
-    group()
-
-    blocks = [slice(at, at + LANES) for at in range(0, width, LANES)]
-    sums = jnp.concatenate([moments[block, :].T for block in blocks], axis=1)
-    kappa = final_curvature(*[sums[q : q + 1, :] for q in range(10)])
-    slot = lax.broadcasted_iota(jnp.int32, (1, width), 1)
-    kappa = jnp.where(slot < count, kappa, 0.0)
-    whole = jnp.concatenate([kappa, jnp.zeros((1, 2 * LANES), jnp.float32)], axis=1)
-    kappa_ref[0] = whole[:, :SLOTS]
-
-    sub = lax.broadcasted_iota(jnp.int32, (ROWS, width), 0)
-    spread = jnp.where(sub == (row[0:1, :width] >> 7), SIGMA * kappa, 0.0)
-    total = jnp.zeros((ROWS, LANES), jnp.float32)
-    for piece in pieces(spread):
-        for block in blocks:
-            end = min(block.stop, SLOTS)
-            total = total + jnp.dot(
-                piece[:, block.start : end],
-                hot[1, SLOTS + block.start : SLOTS + end, :LANES],
-                preferred_element_type=jnp.float32,
-            )
-    added[...] = total
+    turned = [moments[at : at + LANES, :].T[0:1] for at in range(0, width, LANES)]
+    turned = jnp.concatenate(turned + [jnp.zeros((1, 2 * LANES), jnp.float32)], axis=1)
+    kappa_ref[0] = turned[:, :SLOTS]
 
 
 def curvature_kernel(
@@ -190,8 +180,9 @@
 
     count = counts_ref[0, 0]
     rest = (codes_ref, kappa_ref, table, hot, window, place, row, moments, added)
-    pl.when(count <= FEW)(lambda: curvature_of(FEW, count, *rest))
-    pl.when(count > FEW)(lambda: curvature_of(SLOTS, count, *rest))
+    pl.when(count <= SIZES[0])(lambda: curvature_of(SIZES[0], count, *rest))
+    pl.when((count > SIZES[0]) & (count <= SIZES[1]))(lambda: curvature_of(SIZES[1], count, *rest))
+    pl.when(count > SIZES[1])(lambda: curvature_of(SLOTS, count, *rest))
 
     rhs = source_ref[...] + added[...].reshape(8, 8, LANES)
     rhs_ref[...] = rhs

time: 20.9 us -> 20.5 us (0.981)
  starting transfers between devices: 5.57 us -> 7.3 us
  Pallas kernels: 3.92 us -> 2.72 us
  waiting for transfers between devices: 3.32 us -> 2.18 us
  blocking collectives: 6.56 us -> 6.84 us
    ppermute x2, starting transfers between devices: 5.57 us -> 7.3 us  [swap_odd(): return lax.ppermute(value, axis, pairs)]
    pallas_call x1, Pallas kernels: 3 us -> 1.81 us  [curvature_call(): pl.pallas_call(curvature_kernel, out_shape=(jax.ShapeDtypeStruct((1, 1, S...]
    ppermute x2, waiting for transfers between devices: 3.32 us -> 2.18 us  [swap_odd(): return lax.ppermute(value, axis, pairs)]
    all_gather x2, blocking collectives: 6.56 us -> 6.84 us  [gather_even(): return lax.all_gather(value, axis, axis=0, axis_index_groups=groups)]
where the time goes in v7:
time: 20.5 us; the launch traced here: 20.3 us
  starting transfers between devices  7.3 us (36%)
  blocking collectives  6.84 us (33%)
  Pallas kernels  2.72 us (13%)
  waiting for transfers between devices  2.18 us (11%)
  between operations  1.31 us (6%)
    ppermute x2, starting transfers between devices, swap_odd(): return lax.ppermute(value, axis, pairs)  7.3 us
    all_gather x2, blocking collectives, gather_even(): return lax.all_gather(value, axis, axis=0, axis_index_groups=groups)  6.84 us
    ppermute x2, waiting for transfers between devices, swap_odd(): return lax.ppermute(value, axis, pairs)  2.18 us
    pallas_call x1, Pallas kernels, curvature_call(): pl.pallas_call(curvature_kernel, out_shape=(jax.ShapeDtypeStruct((1, 1, S...  1.81 us
    pallas_call x1, Pallas kernels, sweeps_call(): pl.pallas_call(functools.partial(sweeps_kernel, n_gx, n_gy), out_shape=(j...  0.87 us
  transfers between devices with their start and end apart: 2, of which 1 were waited for; matrix products, arithmetic and copies ran while one was open for 0% of the time, Pallas kernels for 0%

profile of v7, /device:TPU:258, one launch (start us, length us, event | category | flops | bytes accessed | tf_op | source)
XLA Modules:
  0.0 20.3 jit_solution(10626429642324738364)
XLA Ops:
  1.3 1.8 %curvature.1 = (f32[1,1,192]{2,1,0:T(1,128)S(1)}, f32[8,8,128]{2,1,0:T(8,128)S(1)}, f32[8,8,128]{2,1,0:T(8,128)S(1)}, f32[5,8,128]{2,1,0:T(8,128)S(1)}, f32[5,8,128]{2,1,0:T(8,128)S(1)}) custom-call(f32[3,8,8,128]{3,2,1,0:T(8,128)} %jitter_hbm.1, f32[8,8,128]{2,1,0:T(8,128)} %colour_hbm.1, s32[1,1,192]{2,1,0:T(1,128)} %cells_hbm.1, ...), custom_call_target="tpu_custom_call" | custom-call | tf_op jit(solution)/shard_map/curvature/pallas_call | solution.py:206
  3.1 3.9 %collective-permute-start = (f32[5,8,128]{2,1,0:T(8,128)S(1)}, f32[5,8,128]{2,1,0:T(8,128)S(1)}, u32[]{:S(2)}, u32[]{:S(2)}) collective-permute-start(f32[5,8,128]{2,1,0:T(8,128)S(1)} %get-tuple-element.13), channel_id=1, source_target_pairs={{4,8},{8,4},{12,16},{16,12},{20,24},{24,20},{28,32},{32,28},{36,40... | collective-permute-start | bytes 61448 | tf_op jit(solution)/shard_map/ppermute | solution.py:341
  7.0 2.3 %all-gather = f32[10,8,128]{2,1,0:T(8,128)S(1)} all-gather(f32[5,8,128]{2,1,0:T(8,128)S(1)} %get-tuple-element.12), channel_id=2, replica_groups={{0,4},{8,12},{16,20},{24,28},{32,36},{40,44},{48,52},{56,60},{64,68},{7..., dimensions={0}, use_global_device_ids=true | all-gather | bytes 61440 | tf_op jit(solution)/shard_map/all_gather | solution.py:346
  9.3 2.2 %collective-permute-done.xo_ref = f32[5,8,128]{2,1,0:T(8,128)S(1)} collective-permute-done((f32[5,8,128]{2,1,0:T(8,128)S(1)}, f32[5,8,128]{2,1,0:T(8,128)S(1)}, u32[]{:S(2)}, u32[]{:S(2)}) %collective-permute-start) | collective-permute-done | bytes 20512 | tf_op jit(solution)/shard_map/ppermute | solution.py:341
  11.6 3.4 %collective-permute-start.1 = (f32[6,8,128]{2,1,0:T(8,128)S(1)}, f32[6,8,128]{2,1,0:T(8,128)S(1)}, u32[]{:S(2)}, u32[]{:S(2)}) collective-permute-start(f32[6,8,128]{2,1,0:T(8,128)S(1)} %get-tuple-element.15), channel_id=1, source_target_pairs={{1,2},{2,1},{5,6},{6,5},{9,10},{10,9},{13,14},{14,13},{17,18},{18,... | collective-permute-start | bytes 73736 | tf_op jit(solution)/shard_map/ppermute | solution.py:341
  15.0 4.5 %all-gather.1 = f32[12,8,128]{2,1,0:T(8,128)S(1)} all-gather(f32[6,8,128]{2,1,0:T(8,128)S(1)} %get-tuple-element.14), channel_id=3, replica_groups={{0,1},{2,3},{4,5},{6,7},{8,9},{10,11},{12,13},{14,15},{16,17},{18,19},{..., dimensions={0}, use_global_device_ids=true | all-gather | bytes 73728 | tf_op jit(solution)/shard_map/all_gather | solution.py:346
  19.5 0.0 collective-permute-done.1.yo_ref
  19.5 0.9 %sweeps.1 = (f32[8,8,128]{2,1,0:T(8,128)}, f32[1,1,192]{2,1,0:T(1,128)}) custom-call(f32[1,1,192]{2,1,0:T(1,128)S(1)} %get-tuple-element.9.kappa_ref, f32[8,8,128]{2,1,0:T(8,128)S(1)} %get-tuple-element.10.pressure_ref, f32[8,8,128]{2,1,0:T(8,128)S(1)} %get-tuple-element.11.rhs_ref, f32[2,5,8,128]{3,2,1,0:T(8,128)S(1)} %bitcast.3, ...), custom_call_target="tpu_custom_call" | custom-call | tf_op jit(solution)/shard_map/sweeps/pallas_call | solution.py:320
  (1 shorter events, 0.0 us)
Async XLA Ops:
  3.1 8.4 %collective-permute-start = (f32[5,8,128]{2,1,0:T(8,128)S(1)}, f32[5,8,128]{2,1,0:T(8,128)S(1)}, u32[]{:S(2)}, u32[]{:S(2)}) collective-permute-start(f32[5,8,128]{2,1,0:T(8,128)S(1)} %get-tuple-element.13), channel_id=1, source_target_pairs={{4,8},{8,4},{12,16},{16,12},{20,24},{24,20},{28,32},{32,28},{36,40... | collective-permute-start | bytes 61448 | tf_op jit(solution)/shard_map/ppermute | solution.py:341
  11.6 7.9 %collective-permute-start.1 = (f32[6,8,128]{2,1,0:T(8,128)S(1)}, f32[6,8,128]{2,1,0:T(8,128)S(1)}, u32[]{:S(2)}, u32[]{:S(2)}) collective-permute-start(f32[6,8,128]{2,1,0:T(8,128)S(1)} %get-tuple-element.15), channel_id=1, source_target_pairs={{1,2},{2,1},{5,6},{6,5},{9,10},{10,9},{13,14},{14,13},{17,18},{18,... | collective-permute-start | bytes 73736 | tf_op jit(solution)/shard_map/ppermute | solution.py:341
